TPU v7x, 32 devices: a whole 2x2x4 slice. The times are simulated.
32 devices in a mesh: section: 2 (over y), batch: 16 (over z, x, core).
Axes of the slice: x: 2, y: 2, z: 4, core: 2. Of those that a mesh axis runs over, the one named last changes fastest.
Arguments:
- images: bfloat16 [32, 64, 3072], P('batch', None, 'section'), may hold values from -1 to 1
- noise_draw: bfloat16 [32, 64, 3072], P('batch', None, 'section'), may hold values from -6 to 6
- cotangent: bfloat16 [32, 64, 3072], P('batch', None, 'section'), may hold values from -6 to 6
- hue_angle: float32 [32], P('batch'), may hold values from -0.5 to 0.5
- saturation: float32 [32], P('batch'), may hold values from 0.5 to 1.5
- timestep: int32 [32], P('batch'), may hold values from 50 to 199
- stem_weight: bfloat16 [3072, 1024], P('section'), may hold values from -0.109375 to 0.109375
- conv_weight: bfloat16 [2, 9216, 1024], P('section', 'batch'), may hold values from -0.0625 to 0.0625
- emb_weight: bfloat16 [2, 1024, 2048], P('section'), may hold values from -0.1875 to 0.1875
- head_weight: bfloat16 [1024, 3072], P(None, 'section'), may hold values from -0.1875 to 0.1875
Outputs:
- purified: bfloat16 [32, 64, 3072], P('batch', None, 'section')
- colour_grad: float32 [32, 2], P('batch')
All inputs are finite; a program needn't handle non-finite values.
Results may differ from a plain program's by a relative error of at most 0.039.
Values may be sent and summed in bfloat16 or wider, within the bound.
A program may use at most 128 MiB of HBM per device.

v0:
```python
import math

import jax
import jax.numpy as jnp
from jax import lax
from jax.sharding import PartitionSpec as P

CH = 1024
GROUPS = 32
TEMB = 1024
GRID = 8
TSTEPS = 1000
PV = 3072


def shifted(value, axis, steps):
    count = lax.axis_size(axis)
    pairs = [(source, (source + steps) % count) for source in range(count)]
    return lax.ppermute(value, axis, pairs)


def from_root(block, axis, holder):
    block = jnp.where(lax.axis_index(axis) == holder, block, jnp.zeros_like(block))
    return lax.psum(block, axis)


def noise_levels(timestep):
    beta_rates = jnp.linspace(0.0001, 0.02, TSTEPS, dtype=jnp.float32)
    levels = jnp.cumprod(1.0 - beta_rates)
    chosen = jnp.arange(TSTEPS, dtype=jnp.int32)[None, :] == timestep[:, None]
    return jnp.sum(jnp.where(chosen, levels[None, :], jnp.float32(0.0)), axis=1)


def time_features(timestep):
    half_width = TEMB // 2
    frequency = jnp.exp(-math.log(10000.0) * jnp.arange(half_width, dtype=jnp.float32) / half_width)
    angles = timestep.astype(jnp.float32)[:, None] * frequency[None, :]
    return jax.nn.silu(jnp.concatenate([jnp.cos(angles), jnp.sin(angles)], axis=1)).astype(
        jnp.bfloat16
    )


def colour_maps(hue_angle, saturation):
    grey_map = jnp.full((3, 3), 1.0 / 3.0, dtype=jnp.float32)
    rotate_map = jnp.eye(3, dtype=jnp.float32) - grey_map
    cross_map = jnp.array(
        [[0.0, -1.0, 1.0], [1.0, 0.0, -1.0], [-1.0, 1.0, 0.0]], dtype=jnp.float32
    ) / math.sqrt(3.0)
    cosine = jnp.cos(hue_angle)[:, None, None]
    sine_of = jnp.sin(hue_angle)[:, None, None]
    turning = cosine * rotate_map + sine_of * cross_map
    sat_scale = saturation[:, None, None]
    matrix = grey_map + sat_scale * turning
    hue_slope = sat_scale * (cosine * cross_map - sine_of * rotate_map)
    return (matrix, hue_slope, turning)


def apply_map(matrix, pixels):
    return jnp.sum(matrix[:, None, None, :, :] * pixels[:, :, :, None, :], axis=-1)


def conv_branch(feature, weight, scaling):
    number = feature.shape[0]
    channels = feature.shape[2]
    grouped = feature.reshape(number, GRID * GRID, GROUPS, channels // GROUPS)
    centre = jnp.mean(grouped, axis=(1, 3), keepdims=True)
    spread_sq = jnp.mean(jnp.square(grouped - centre), axis=(1, 3), keepdims=True)
    normed = ((grouped - centre) * lax.rsqrt(spread_sq + 1e-05)).reshape(
        number, GRID * GRID, channels
    )
    factor = scaling[:, None, :channels]
    offset = scaling[:, None, channels:]
    active = jax.nn.silu(normed * (1.0 + factor) + offset).astype(jnp.bfloat16)
    padded = jnp.pad(active.reshape(number, GRID, GRID, channels), ((0, 0), (1, 1), (1, 1), (0, 0)))
    taps = [
        padded[:, row_tap : row_tap + GRID, col_tap : col_tap + GRID, :]
        for row_tap in range(3)
        for col_tap in range(3)
    ]
    columns = jnp.concatenate(taps, axis=-1).reshape(number * GRID * GRID, 9 * channels)
    product = jnp.dot(columns, weight, preferred_element_type=jnp.float32)
    return product.reshape(number, GRID * GRID, channels)


def residual_block(feature, weight, scaling):
    primal = feature.astype(jnp.float32)
    return (primal + conv_branch(primal, weight, scaling)).astype(jnp.bfloat16)


def block_adjoint(feature, weight, scaling, upstream):
    primal = feature.astype(jnp.float32)

    def branch_only(probe):
        return conv_branch(probe, weight, scaling)

    _, pullback = jax.vjp(branch_only, primal)
    upstream_f = upstream.astype(jnp.float32)
    return (upstream_f + pullback(upstream_f)[0]).astype(jnp.bfloat16)


def section_total(partial_sum):
    return lax.psum(partial_sum.astype(jnp.bfloat16), "section").astype(jnp.float32)


def send_forward(value):
    return shifted(value, "section", 1)


def send_backward(value):
    return shifted(value, "section", -1)


def spread(value, owner):
    return from_root(value, "section", owner)


def store_one(buffer, value, index_at, is_live):
    previous = lax.dynamic_index_in_dim(buffer, index_at, 0, keepdims=False)
    return lax.dynamic_update_index_in_dim(buffer, jnp.where(is_live, value, previous), index_at, 0)


def run_chain(position, entering, worker, sender):
    number = entering.shape[0]
    clocks = number + lax.axis_size("section") - 1

    def advance(clock, state_in):
        incoming, sources, results = state_in
        member = clock - position
        is_live = (member >= 0) & (member < number)
        index_at = jnp.clip(member, 0, number - 1)
        entry_row = lax.dynamic_index_in_dim(entering, index_at, 0, keepdims=False)
        source = jnp.where(position == 0, entry_row, incoming)

        def run_work():
            return worker(source, index_at)

        def pass_through():
            return source

        result = lax.cond(is_live, run_work, pass_through)
        sources = store_one(sources, source, index_at, is_live)
        results = store_one(results, result, index_at, is_live)
        return (sender(result), sources, results)

    start = (jnp.zeros_like(entering[0]), jnp.zeros_like(entering), jnp.zeros_like(entering))
    final_state = lax.fori_loop(0, clocks, advance, start)
    return (final_state[1], final_state[2])


def local(
    images,
    noise_draw,
    cotangent,
    hue_angle,
    saturation,
    timestep,
    stem_weight,
    conv_weight,
    emb_weight,
    head_weight,
):
    sections = lax.axis_size("section")
    place = lax.axis_index("section")
    number = images.shape[0]
    columns_here = images.shape[2]
    full_conv = lax.all_gather(conv_weight, "batch", axis=1, tiled=True)[0]
    level = noise_levels(timestep)
    root_level = jnp.sqrt(level)[:, None, None]
    root_noise = jnp.sqrt(1.0 - level)[:, None, None]
    matrix, hue_slope, sat_slope = colour_maps(hue_angle, saturation)
    pixels = images.astype(jnp.float32).reshape(number, GRID * GRID, columns_here // 3, 3)
    coloured = apply_map(matrix, pixels).reshape(number, GRID * GRID, columns_here)
    noised = root_level * coloured + root_noise * noise_draw.astype(jnp.float32)
    entry_part = jnp.dot(
        noised.astype(jnp.bfloat16).reshape(-1, columns_here),
        stem_weight,
        preferred_element_type=jnp.float32,
    )
    first = section_total(entry_part).astype(jnp.bfloat16).reshape(number, GRID * GRID, CH)
    offsets = jnp.dot(time_features(timestep), emb_weight[0], preferred_element_type=jnp.float32)

    def forward_work(source, index_at):
        scaling = lax.dynamic_slice_in_dim(offsets, index_at, 1, 0)
        return residual_block(source[None], full_conv, scaling)[0]

    fwd_inputs, fwd_outputs = run_chain(place, first, forward_work, send_forward)
    finals = spread(fwd_outputs, sections - 1)
    predicted = jnp.dot(finals.reshape(-1, CH), head_weight, preferred_element_type=jnp.float32)
    predicted = predicted.reshape(number, GRID * GRID, columns_here)
    purified = ((noised - root_noise * predicted) / root_level).astype(jnp.bfloat16)
    weighted = cotangent.astype(jnp.float32) * (1.0 / math.sqrt(GRID * GRID * PV))
    eps_grad = (-(root_noise / root_level) * weighted).astype(jnp.bfloat16)
    seed_part = lax.dot_general(
        eps_grad.reshape(-1, columns_here),
        head_weight,
        (((1,), (1,)), ((), ())),
        preferred_element_type=jnp.float32,
    )
    seed = section_total(seed_part).astype(jnp.bfloat16).reshape(number, GRID * GRID, CH)

    def adjoint_work(source, index_at):
        saved = lax.dynamic_index_in_dim(fwd_inputs, index_at, 0, keepdims=True)
        scaling = lax.dynamic_slice_in_dim(offsets, index_at, 1, 0)
        return block_adjoint(saved, full_conv, scaling, source[None])[0]

    back_inputs, back_outputs = run_chain(sections - 1 - place, seed, adjoint_work, send_backward)
    grads = spread(back_outputs, 0)
    stem_back = lax.dot_general(
        grads.reshape(-1, CH),
        stem_weight,
        (((1,), (1,)), ((), ())),
        preferred_element_type=jnp.float32,
    )
    stem_back = stem_back.reshape(number, GRID * GRID, columns_here)
    pixel_grad = (weighted + root_level * stem_back).reshape(
        number, GRID * GRID, columns_here // 3, 3
    )
    hue_part = jnp.sum(pixel_grad * apply_map(hue_slope, pixels), axis=(1, 2, 3))
    sat_part = jnp.sum(pixel_grad * apply_map(sat_slope, pixels), axis=(1, 2, 3))
    colour_grad = section_total(jnp.stack([hue_part, sat_part], axis=1))
    return (purified, colour_grad)


def solution(mesh):
    in_specs = (
        P("batch", None, "section"),
        P("batch", None, "section"),
        P("batch", None, "section"),
        P("batch"),
        P("batch"),
        P("batch"),
        P("section", None),
        P("section", "batch", None),
        P("section", None, None),
        P(None, "section"),
    )
    out_specs = (P("batch", None, "section"), P("batch", None))
    return jax.shard_map(local, mesh=mesh, in_specs=in_specs, out_specs=out_specs, check_vma=False)
```

profile of v0, /device:TPU:0, one launch (start us, length us, event | category | flops | bytes accessed | tf_op | source)
XLA Modules:
  0.0 400.9 jit_solution(12375936215744181771)
XLA Ops:
  12.0 3.4 copy.21
  15.4 3.4 multiply_reduce_fusion.2
  22.2 3.4 copy.23
  34.0 3.4 fusion.58
  37.4 27.4 %all-reduce.18.cloned.1.call-done = (bf16[2,64,1024]{2,1,0:T(8,128)(2,1)}, bf16[2,64,1024]{2,1,0:T(8,128)(2,1)}) async-done(((bf16[2,64,1024]{2,1,0:T(8,128)(2,1)}, bf16[2,64,1024]{2,1,0:T(8,128)(2,1)}), (bf16[2,64,1024]{2,1,0:T(8,128)(2,1)}, bf16[2,64,1024]{2,1,0:T(8,128)(2,1)})) %all-reduce.18.cloned.1.call-update) | async-done | bytes 524304 | tf_op jit(solution)/shard_map/psum | solution.py:102
  64.8 72.1 %all-gather.2.cloned.1.call-done = bf16[1,9216,1024]{2,1,0:T(8,128)(2,1)} async-done(((bf16[1,576,1024]{2,1,0:T(8,128)(2,1)}), bf16[1,9216,1024]{2,1,0:T(8,128)(2,1)}) %all-gather.2.cloned.1.call-update) | async-done | bytes 18874384 | tf_op jit(solution)/shard_map/all_gather | solution.py:166
  138.3 72.6 %while.34 = (s32[]{:T(128)}, bf16[64,1024]{1,0:T(8,128)(2,1)}, bf16[2,64,1024]{2,1,0:T(8,128)(2,1)S(1)}, bf16[2,64,1024]{2,1,0:T(8,128)(2,1)}, s32[]{:T(128)}, /...) while((s32[]{:T(128)}, bf16[64,1024]{1,0:T(8,128)(2,1)}, ...), condition=%wide.region_12.13_spmd, body=%wide.region_5.12_spmd.sunk | while | flops 1210057728 | bytes 25409360 | solution.py:146
  139.3 18.3 %conditional.4 = (bf16[64,1024]{1,0:T(8,128)(2,1)S(1)}) conditional(s32[]{:T(128)} %convert_element_type.245, bf16[64,1024]{1,0:T(8,128)(2,1)S(1)} %get-tuple-element.587, (bf16[64,1024]{1,0:T(8,128)(2,1)S(1)}, s32[]{:T(128)}, f32[2,2048]{1,0:T(2,128)}, bf16[9216,1024]{1,0:T(8,128)(2,1)}) %tuple.116), branch_computations={%region_6.6_spmd, %region_7.11_spmd} | conditional | flops 1209861120 | bytes 23311430 | solution.py:140
  147.8 9.8 %fusion = bf16[64,1024]{1,0:T(8,128)(2,1)S(1)} fusion(bf16[64,9216]{1,0:T(8,128)(2,1)S(1)} %fusion.32, bf16[9216,1024]{1,0:T(8,128)(2,1)} %get-tuple-element.369, bf16[64,1024]{1,0:T(8,128)(2,1)S(1)} %get-tuple-element.366), kind=kOutput, calls=%fused_computation.1 | convolution fusion | flops 1208156160 | bytes 20316160 | tf_op jit(solution)/shard_map/while/body/eval_jaxpr/cond/branch_1_fun/dot_general | solution.py:81
  159.3 4.1 %collective-permute-done = bf16[64,1024]{1,0:T(8,128)(2,1)} collective-permute-done((bf16[64,1024]{1,0:T(8,128)(2,1)S(1)}, bf16[64,1024]{1,0:T(8,128)(2,1)}, u32[]{:S(2)}, u32[]{:S(2)}) %collective-permute-start) | collective-permute-done | bytes 131104 | tf_op jit(solution)/shard_map/while/body/eval_jaxpr/ppermute | solution.py:19
  164.5 18.3 %conditional.4 = (bf16[64,1024]{1,0:T(8,128)(2,1)S(1)}) conditional(s32[]{:T(128)} %convert_element_type.245, bf16[64,1024]{1,0:T(8,128)(2,1)S(1)} %get-tuple-element.587, (bf16[64,1024]{1,0:T(8,128)(2,1)S(1)}, s32[]{:T(128)}, f32[2,2048]{1,0:T(2,128)}, bf16[9216,1024]{1,0:T(8,128)(2,1)}) %tuple.116), branch_computations={%region_6.6_spmd, %region_7.11_spmd} | conditional | flops 1209861120 | bytes 23311430 | solution.py:140
  172.9 9.8 %fusion = bf16[64,1024]{1,0:T(8,128)(2,1)S(1)} fusion(bf16[64,9216]{1,0:T(8,128)(2,1)S(1)} %fusion.32, bf16[9216,1024]{1,0:T(8,128)(2,1)} %get-tuple-element.369, bf16[64,1024]{1,0:T(8,128)(2,1)S(1)} %get-tuple-element.366), kind=kOutput, calls=%fused_computation.1 | convolution fusion | flops 1208156160 | bytes 20316160 | tf_op jit(solution)/shard_map/while/body/eval_jaxpr/cond/branch_1_fun/dot_general | solution.py:81
  188.9 19.0 %collective-permute-start = (bf16[64,1024]{1,0:T(8,128)(2,1)S(1)}, bf16[64,1024]{1,0:T(8,128)(2,1)}, u32[]{:S(2)}, u32[]{:S(2)}) collective-permute-start(bf16[64,1024]{1,0:T(8,128)(2,1)S(1)} %get-tuple-element.674), channel_id=1, source_target_pairs={{0,16},{16,0},{1,17},{17,1},{2,18},{18,2},{3,19},{19,3},{4,20},{20... | collective-permute-start | bytes 393224 | tf_op jit(solution)/shard_map/while/body/eval_jaxpr/ppermute | solution.py:19
  212.3 138.6 %while.35 = (s32[]{:T(128)}, bf16[64,1024]{1,0:T(8,128)(2,1)}, bf16[2,64,1024]{2,1,0:T(8,128)(2,1)}, s32[]{:T(128)}, pred[]{:T(512)}, /*index=5*/bf16[2,64,1024]...) while((s32[]{:T(128)}, bf16[64,1024]{1,0:T(8,128)(2,1)}, ...), condition=%wide.region_28.29_spmd, body=%wide.region_15.28_spmd.sunk | while | flops 1212769664 | bytes 27270924 | solution.py:146
  213.3 42.1 %collective-permute-start.1 = (bf16[64,1024]{1,0:T(8,128)(2,1)S(1)}, bf16[64,1024]{1,0:T(8,128)(2,1)}, u32[]{:S(2)}, u32[]{:S(2)}) collective-permute-start(bf16[64,1024]{1,0:T(8,128)(2,1)S(1)} %get-tuple-element.675), channel_id=1, source_target_pairs={{0,16},{16,0},{1,17},{17,1},{2,18},{18,2},{3,19},{19,3},{4,20},{20... | collective-permute-start | bytes 393224 | tf_op jit(solution)/shard_map/while/body/eval_jaxpr/ppermute | solution.py:19
  259.5 40.1 %conditional.5 = (bf16[64,1024]{1,0:T(8,128)(2,1)S(1)}) conditional(s32[]{:T(128)} %convert_element_type.246, bf16[64,1024]{1,0:T(8,128)(2,1)S(1)} %bitcast_select_fusion.7, (bf16[64,1024]{1,0:T(8,128)(2,1)S(1)}, bf16[9216,1024]{1,0:T(8,128)(2,1)}, s32[]{:T(128)}, bf16[2,64,1024]{2,1,0:T(8,128)(2,1)S(1)}, f32[2,2048]{1,0:T(2,128)}) %tuple.118), branch_computations={%region_16.16_spmd, %region_17.27_spmd} | conditional | flops 1212638592 | bytes 25697282 | solution.py:140
  267.2 13.2 %fusion.33 = bf16[1,8,8,9216]{3,2,1,0:T(8,128)(2,1)} fusion(bf16[64,1024]{1,0:T(8,128)(2,1)S(1)} %get-tuple-element.380, bf16[9216,1024]{1,0:T(8,128)(2,1)} %get-tuple-element.381), kind=kOutput, calls=%fused_computation.57 | convolution fusion | flops 1208549376 | bytes 20185088 | tf_op jit(solution)/shard_map/while/body/eval_jaxpr/cond/branch_1_fun/transpose(jvp())/dot_general | solution.py:81
  305.7 40.1 %conditional.5 = (bf16[64,1024]{1,0:T(8,128)(2,1)S(1)}) conditional(s32[]{:T(128)} %convert_element_type.246, bf16[64,1024]{1,0:T(8,128)(2,1)S(1)} %bitcast_select_fusion.7, (bf16[64,1024]{1,0:T(8,128)(2,1)S(1)}, bf16[9216,1024]{1,0:T(8,128)(2,1)}, s32[]{:T(128)}, bf16[2,64,1024]{2,1,0:T(8,128)(2,1)S(1)}, f32[2,2048]{1,0:T(2,128)}) %tuple.118), branch_computations={%region_16.16_spmd, %region_17.27_spmd} | conditional | flops 1212638592 | bytes 25697282 | solution.py:140
  313.4 13.2 %fusion.33 = bf16[1,8,8,9216]{3,2,1,0:T(8,128)(2,1)} fusion(bf16[64,1024]{1,0:T(8,128)(2,1)S(1)} %get-tuple-element.380, bf16[9216,1024]{1,0:T(8,128)(2,1)} %get-tuple-element.381), kind=kOutput, calls=%fused_computation.57 | convolution fusion | flops 1208549376 | bytes 20185088 | tf_op jit(solution)/shard_map/while/body/eval_jaxpr/cond/branch_1_fun/transpose(jvp())/dot_general | solution.py:81
  347.5 3.4 collective-permute-done.1
  363.3 3.4 copy.27
  366.7 14.6 %all-reduce.16.cloned.1.call-done = (bf16[2,64,1024]{2,1,0:T(8,128)(2,1)}, bf16[2,64,1024]{2,1,0:T(8,128)(2,1)}) async-done(((bf16[2,64,1024]{2,1,0:T(8,128)(2,1)}, bf16[2,64,1024]{2,1,0:T(8,128)(2,1)}), (bf16[2,64,1024]{2,1,0:T(8,128)(2,1)}, bf16[2,64,1024]{2,1,0:T(8,128)(2,1)})) %all-reduce.16.cloned.1.call-update) | async-done | bytes 524304 | tf_op jit(solution)/shard_map/psum | solution.py:24
  381.4 3.8 multiply_reduce_fusion.5
  385.2 4.9 %psum.39 = bf16[2,2]{0,1:T(2,128)(2,1)S(1)} all-reduce(bf16[2,2]{0,1:T(2,128)(2,1)S(1)} %pad_maximum_fusion.1), channel_id=1, replica_groups=mesh['section'=2,'batch'=16] {'section'}, use_global_device_ids=true, to_apply=%region_34.35 | all-reduce | flops 4 | bytes 16 | tf_op jit(solution)/shard_map/psum | solution.py:102
  (197 shorter events, 130.2 us)
Async XLA Ops:
  8.0 23.3 %copy-start = (bf16[1024,1536]{1,0:T(8,128)(2,1)S(1)}, bf16[1024,1536]{1,0:T(8,128)(2,1)}, u32[]{:S(2)}) copy-start(bf16[1024,1536]{1,0:T(8,128)(2,1)} %param.28) | copy-start | bytes 9437188
  8.0 56.8 %all-reduce.18.cloned.1.call-start = ((), (), s32[]{:S(2)}) async-start(), calls=%async_computation.2 | async-start | bytes 1048576 | tf_op jit(solution)/shard_map/psum | solution.py:102
  12.0 3.4 copy-start.6
  12.0 3.4 copy-start.7
  22.2 4.0 %copy-start.8 = (s32[2]{0:T(128)S(1)}, s32[2]{0:T(128)}, u32[]{:S(2)}) copy-start(s32[2]{0:T(128)} %param.24) | copy-start | bytes 28
  26.4 4.8 %copy-start.2 = (f32[2]{0:T(128)}, f32[2]{0:T(128)S(1)}, u32[]{:S(2)}) copy-start(f32[2]{0:T(128)S(1)} %get-tuple-element.477) | copy-start | bytes 28
  26.4 4.8 %copy-start.4 = (f32[2]{0:T(128)}, f32[2]{0:T(128)S(1)}, u32[]{:S(2)}) copy-start(f32[2]{0:T(128)S(1)} %get-tuple-element.479) | copy-start | bytes 28
  33.1 103.8 %all-gather.2.cloned.1.call-start = ((), (), s32[]{:S(2)}) async-start(), calls=%async_computation | async-start | bytes 20054016 | tf_op jit(solution)/shard_map/all_gather | solution.py:166
  33.7 347.6 %all-reduce.16.cloned.1.call-start = ((), (), s32[]{:S(2)}) async-start(), calls=%async_computation.1 | async-start | bytes 1048576 | tf_op jit(solution)/shard_map/psum | solution.py:24
  157.6 5.8 %collective-permute-start = (bf16[64,1024]{1,0:T(8,128)(2,1)S(1)}, bf16[64,1024]{1,0:T(8,128)(2,1)}, u32[]{:S(2)}, u32[]{:S(2)}) collective-permute-start(bf16[64,1024]{1,0:T(8,128)(2,1)S(1)} %get-tuple-element.674), channel_id=1, source_target_pairs={{0,16},{16,0},{1,17},{17,1},{2,18},{18,2},{3,19},{19,3},{4,20},{20... | collective-permute-start | bytes 393224 | tf_op jit(solution)/shard_map/while/body/eval_jaxpr/ppermute | solution.py:19
  182.8 5.1 %collective-permute-start = (bf16[64,1024]{1,0:T(8,128)(2,1)S(1)}, bf16[64,1024]{1,0:T(8,128)(2,1)}, u32[]{:S(2)}, u32[]{:S(2)}) collective-permute-start(bf16[64,1024]{1,0:T(8,128)(2,1)S(1)} %get-tuple-element.674), channel_id=1, source_target_pairs={{0,16},{16,0},{1,17},{17,1},{2,18},{18,2},{3,19},{19,3},{4,20},{20... | collective-permute-start | bytes 393224 | tf_op jit(solution)/shard_map/while/body/eval_jaxpr/ppermute | solution.py:19
  188.9 22.0 %collective-permute-start = (bf16[64,1024]{1,0:T(8,128)(2,1)S(1)}, bf16[64,1024]{1,0:T(8,128)(2,1)}, u32[]{:S(2)}, u32[]{:S(2)}) collective-permute-start(bf16[64,1024]{1,0:T(8,128)(2,1)S(1)} %get-tuple-element.674), channel_id=1, source_target_pairs={{0,16},{16,0},{1,17},{17,1},{2,18},{18,2},{3,19},{19,3},{4,20},{20... | collective-permute-start | bytes 393224 | tf_op jit(solution)/shard_map/while/body/eval_jaxpr/ppermute | solution.py:19
  213.3 45.2 %collective-permute-start.1 = (bf16[64,1024]{1,0:T(8,128)(2,1)S(1)}, bf16[64,1024]{1,0:T(8,128)(2,1)}, u32[]{:S(2)}, u32[]{:S(2)}) collective-permute-start(bf16[64,1024]{1,0:T(8,128)(2,1)S(1)} %get-tuple-element.675), channel_id=1, source_target_pairs={{0,16},{16,0},{1,17},{17,1},{2,18},{18,2},{3,19},{19,3},{4,20},{20... | collective-permute-start | bytes 393224 | tf_op jit(solution)/shard_map/while/body/eval_jaxpr/ppermute | solution.py:19
  265.2 0.5 copy-start.1
  299.6 5.1 %collective-permute-start.1 = (bf16[64,1024]{1,0:T(8,128)(2,1)S(1)}, bf16[64,1024]{1,0:T(8,128)(2,1)}, u32[]{:S(2)}, u32[]{:S(2)}) collective-permute-start(bf16[64,1024]{1,0:T(8,128)(2,1)S(1)} %get-tuple-element.675), channel_id=1, source_target_pairs={{0,16},{16,0},{1,17},{17,1},{2,18},{18,2},{3,19},{19,3},{4,20},{20... | collective-permute-start | bytes 393224 | tf_op jit(solution)/shard_map/while/body/eval_jaxpr/ppermute | solution.py:19
  311.4 0.5 copy-start.1
  345.8 5.1 %collective-permute-start.1 = (bf16[64,1024]{1,0:T(8,128)(2,1)S(1)}, bf16[64,1024]{1,0:T(8,128)(2,1)}, u32[]{:S(2)}, u32[]{:S(2)}) collective-permute-start(bf16[64,1024]{1,0:T(8,128)(2,1)S(1)} %get-tuple-element.675), channel_id=1, source_target_pairs={{0,16},{16,0},{1,17},{17,1},{2,18},{18,2},{3,19},{19,3},{4,20},{20... | collective-permute-start | bytes 393224 | tf_op jit(solution)/shard_map/while/body/eval_jaxpr/ppermute | solution.py:19
  363.3 18.0 %copy-start.3 = (f32[2]{0:T(128)S(1)}, f32[2]{0:T(128)}, u32[]{:S(2)}) copy-start(f32[2]{0:T(128)} %copy-done.2) | copy-start | bytes 28
  381.4 9.4 %copy-start.5 = (f32[2]{0:T(128)S(1)}, f32[2]{0:T(128)}, u32[]{:S(2)}) copy-start(f32[2]{0:T(128)} %copy-done.4) | copy-start | bytes 28
Sparse Core Ops, SparseCore 0:
  33.3 31.5 all-reduce.17
  353.5 27.8 all-reduce.15
Sparse Core Ops, SparseCore 1:
  35.3 101.6 all-gather.1
where the time goes:
time: 404 us; the launch traced here: 401 us
  waiting for transfers between devices  130 us (32%)
  local copies, waits for them, and re-layouts  72.5 us (18%)
  starting transfers between devices  63.8 us (16%)
  matrix products  61.1 us (15%)
  other arithmetic  52.8 us (13%)
  between operations  15.6 us (4%)
  blocking collectives  4.94 us (1%)
    all_gather x1, waiting for transfers between devices, local(): full_conv = lax.all_gather(conv_weight, 'batch', axis=1, tiled=True)[0]  72.1 us
    ppermute x6, starting transfers between devices, shifted(): return lax.ppermute(value, axis, pairs)  63.6 us
    dot_general x4, matrix products, conv_branch(): product = jnp.dot(columns, weight, preferred_element_type=jnp.float32)  46.1 us
    psum x1, waiting for transfers between devices, section_total(): lax.psum(partial_sum.astype(jnp.bfloat16), 'section').astype(jnp.float32)  27.4 us
    reduce_sum x5, local copies, waits for them, and re-layouts, apply_map(): jnp.sum(matrix[:, None, None, :, :] * pixels[:, :, :, None, :], axis=-1)  16.7 us
    ppermute x6, waiting for transfers between devices, shifted(): return lax.ppermute(value, axis, pairs)  15.1 us
    psum x1, waiting for transfers between devices, from_root(): return lax.psum(block, axis)  14.6 us
    reduce_sum x8, other arithmetic, conv_branch(): grouped - centre  11.6 us
  transfers between devices with their start and end apart: 9, of which 9 were waited for; matrix products, arithmetic and copies ran while one was open for 7% of the time, Pallas kernels for 0%

commit v1 on v0

--- a/solution.py
+++ b/solution.py
@@ -26,9 +26,8 @@
 
 def noise_levels(timestep):
     beta_rates = jnp.linspace(0.0001, 0.02, TSTEPS, dtype=jnp.float32)
-    levels = jnp.cumprod(1.0 - beta_rates)
-    chosen = jnp.arange(TSTEPS, dtype=jnp.int32)[None, :] == timestep[:, None]
-    return jnp.sum(jnp.where(chosen, levels[None, :], jnp.float32(0.0)), axis=1)
+    steps = jnp.arange(TSTEPS, dtype=jnp.int32)[None, :]
+    return jnp.prod(jnp.where(steps <= timestep[:, None], 1.0 - beta_rates[None, :], 1.0), axis=1)
 
 
 def time_features(timestep):

time: 404 us -> 403 us (level)
  no operation moved by 1% of the time
where the time goes in v1:
time: 403 us; the launch traced here: 400 us
  waiting for transfers between devices  130 us (32%)
  local copies, waits for them, and re-layouts  72.3 us (18%)
  starting transfers between devices  63.8 us (16%)
  matrix products  61.1 us (15%)
  other arithmetic  52.4 us (13%)
  between operations  15.6 us (4%)
  blocking collectives  4.94 us (1%)
    all_gather x1, waiting for transfers between devices, local(): full_conv = lax.all_gather(conv_weight, 'batch', axis=1, tiled=True)[0]  72.1 us
    ppermute x6, starting transfers between devices, shifted(): return lax.ppermute(value, axis, pairs)  63.7 us
    dot_general x4, matrix products, conv_branch(): product = jnp.dot(columns, weight, preferred_element_type=jnp.float32)  46.1 us
    psum x1, waiting for transfers between devices, section_total(): lax.psum(partial_sum.astype(jnp.bfloat16), 'section').astype(jnp.float32)  27.4 us
    reduce_sum x5, local copies, waits for them, and re-layouts, apply_map(): jnp.sum(matrix[:, None, None, :, :] * pixels[:, :, :, None, :], axis=-1)  16.7 us
    ppermute x6, waiting for transfers between devices, shifted(): return lax.ppermute(value, axis, pairs)  15.1 us
    psum x1, waiting for transfers between devices, from_root(): return lax.psum(block, axis)  14.6 us
    reduce_sum x8, other arithmetic, conv_branch(): grouped - centre  11.6 us
  transfers between devices with their start and end apart: 9, of which 9 were waited for; matrix products, arithmetic and copies ran while one was open for 7% of the time, Pallas kernels for 0%

profile of v1, /device:TPU:0, one launch (start us, length us, event | category | flops | bytes accessed | tf_op | source)
XLA Modules:
  0.0 400.3 jit_solution(12848415910830775743)
XLA Ops:
  12.0 3.4 copy.21
  15.4 3.4 multiply_reduce_fusion.2
  22.2 3.4 copy.23
  33.4 3.4 fusion.58
  36.8 27.4 %all-reduce.17.cloned.1.call-done = (bf16[2,64,1024]{2,1,0:T(8,128)(2,1)}, bf16[2,64,1024]{2,1,0:T(8,128)(2,1)}) async-done(((bf16[2,64,1024]{2,1,0:T(8,128)(2,1)}, bf16[2,64,1024]{2,1,0:T(8,128)(2,1)}), (bf16[2,64,1024]{2,1,0:T(8,128)(2,1)}, bf16[2,64,1024]{2,1,0:T(8,128)(2,1)})) %all-reduce.17.cloned.1.call-update) | async-done | bytes 524304 | tf_op jit(solution)/shard_map/psum | solution.py:101
  64.2 72.1 %all-gather.2.cloned.1.call-done = bf16[1,9216,1024]{2,1,0:T(8,128)(2,1)} async-done(((bf16[1,576,1024]{2,1,0:T(8,128)(2,1)}), bf16[1,9216,1024]{2,1,0:T(8,128)(2,1)}) %all-gather.2.cloned.1.call-update) | async-done | bytes 18874384 | tf_op jit(solution)/shard_map/all_gather | solution.py:165
  137.7 72.6 %while.34 = (s32[]{:T(128)}, bf16[64,1024]{1,0:T(8,128)(2,1)}, bf16[2,64,1024]{2,1,0:T(8,128)(2,1)S(1)}, bf16[2,64,1024]{2,1,0:T(8,128)(2,1)}, s32[]{:T(128)}, /...) while((s32[]{:T(128)}, bf16[64,1024]{1,0:T(8,128)(2,1)}, ...), condition=%wide.region_10.11_spmd, body=%wide.region_3.10_spmd.sunk | while | flops 1210057728 | bytes 25409360 | solution.py:145
  138.7 18.3 %conditional.4 = (bf16[64,1024]{1,0:T(8,128)(2,1)S(1)}) conditional(s32[]{:T(128)} %convert_element_type.245, bf16[64,1024]{1,0:T(8,128)(2,1)S(1)} %get-tuple-element.587, (bf16[64,1024]{1,0:T(8,128)(2,1)S(1)}, s32[]{:T(128)}, f32[2,2048]{1,0:T(2,128)}, bf16[9216,1024]{1,0:T(8,128)(2,1)}) %tuple.116), branch_computations={%region_4.4_spmd, %region_5.9_spmd} | conditional | flops 1209861120 | bytes 23311430 | solution.py:139
  147.2 9.8 %fusion = bf16[64,1024]{1,0:T(8,128)(2,1)S(1)} fusion(bf16[64,9216]{1,0:T(8,128)(2,1)S(1)} %fusion.32, bf16[9216,1024]{1,0:T(8,128)(2,1)} %get-tuple-element.369, bf16[64,1024]{1,0:T(8,128)(2,1)S(1)} %get-tuple-element.366), kind=kOutput, calls=%fused_computation.1 | convolution fusion | flops 1208156160 | bytes 20316160 | tf_op jit(solution)/shard_map/while/body/eval_jaxpr/cond/branch_1_fun/dot_general | solution.py:80
  158.7 4.1 %collective-permute-done = bf16[64,1024]{1,0:T(8,128)(2,1)} collective-permute-done((bf16[64,1024]{1,0:T(8,128)(2,1)S(1)}, bf16[64,1024]{1,0:T(8,128)(2,1)}, u32[]{:S(2)}, u32[]{:S(2)}) %collective-permute-start) | collective-permute-done | bytes 131104 | tf_op jit(solution)/shard_map/while/body/eval_jaxpr/ppermute | solution.py:19
  163.9 18.3 %conditional.4 = (bf16[64,1024]{1,0:T(8,128)(2,1)S(1)}) conditional(s32[]{:T(128)} %convert_element_type.245, bf16[64,1024]{1,0:T(8,128)(2,1)S(1)} %get-tuple-element.587, (bf16[64,1024]{1,0:T(8,128)(2,1)S(1)}, s32[]{:T(128)}, f32[2,2048]{1,0:T(2,128)}, bf16[9216,1024]{1,0:T(8,128)(2,1)}) %tuple.116), branch_computations={%region_4.4_spmd, %region_5.9_spmd} | conditional | flops 1209861120 | bytes 23311430 | solution.py:139
  172.4 9.8 %fusion = bf16[64,1024]{1,0:T(8,128)(2,1)S(1)} fusion(bf16[64,9216]{1,0:T(8,128)(2,1)S(1)} %fusion.32, bf16[9216,1024]{1,0:T(8,128)(2,1)} %get-tuple-element.369, bf16[64,1024]{1,0:T(8,128)(2,1)S(1)} %get-tuple-element.366), kind=kOutput, calls=%fused_computation.1 | convolution fusion | flops 1208156160 | bytes 20316160 | tf_op jit(solution)/shard_map/while/body/eval_jaxpr/cond/branch_1_fun/dot_general | solution.py:80
  188.3 19.0 %collective-permute-start = (bf16[64,1024]{1,0:T(8,128)(2,1)S(1)}, bf16[64,1024]{1,0:T(8,128)(2,1)}, u32[]{:S(2)}, u32[]{:S(2)}) collective-permute-start(bf16[64,1024]{1,0:T(8,128)(2,1)S(1)} %get-tuple-element.674), channel_id=1, source_target_pairs={{0,16},{16,0},{1,17},{17,1},{2,18},{18,2},{3,19},{19,3},{4,20},{20... | collective-permute-start | bytes 393224 | tf_op jit(solution)/shard_map/while/body/eval_jaxpr/ppermute | solution.py:19
  211.7 138.6 %while.35 = (s32[]{:T(128)}, bf16[64,1024]{1,0:T(8,128)(2,1)}, bf16[2,64,1024]{2,1,0:T(8,128)(2,1)}, s32[]{:T(128)}, pred[]{:T(512)}, /*index=5*/bf16[2,64,1024]...) while((s32[]{:T(128)}, bf16[64,1024]{1,0:T(8,128)(2,1)}, ...), condition=%wide.region_26.27_spmd, body=%wide.region_13.26_spmd.sunk | while | flops 1212769664 | bytes 27270924 | solution.py:145
  212.7 42.1 %collective-permute-start.1 = (bf16[64,1024]{1,0:T(8,128)(2,1)S(1)}, bf16[64,1024]{1,0:T(8,128)(2,1)}, u32[]{:S(2)}, u32[]{:S(2)}) collective-permute-start(bf16[64,1024]{1,0:T(8,128)(2,1)S(1)} %get-tuple-element.675), channel_id=1, source_target_pairs={{0,16},{16,0},{1,17},{17,1},{2,18},{18,2},{3,19},{19,3},{4,20},{20... | collective-permute-start | bytes 393224 | tf_op jit(solution)/shard_map/while/body/eval_jaxpr/ppermute | solution.py:19
  258.9 40.1 %conditional.5 = (bf16[64,1024]{1,0:T(8,128)(2,1)S(1)}) conditional(s32[]{:T(128)} %convert_element_type.246, bf16[64,1024]{1,0:T(8,128)(2,1)S(1)} %bitcast_select_fusion.7, (bf16[64,1024]{1,0:T(8,128)(2,1)S(1)}, bf16[9216,1024]{1,0:T(8,128)(2,1)}, s32[]{:T(128)}, bf16[2,64,1024]{2,1,0:T(8,128)(2,1)S(1)}, f32[2,2048]{1,0:T(2,128)}) %tuple.118), branch_computations={%region_14.14_spmd, %region_15.0_spmd} | conditional | flops 1212638592 | bytes 25697282 | solution.py:139
  266.6 13.2 %fusion.33 = bf16[1,8,8,9216]{3,2,1,0:T(8,128)(2,1)} fusion(bf16[64,1024]{1,0:T(8,128)(2,1)S(1)} %get-tuple-element.380, bf16[9216,1024]{1,0:T(8,128)(2,1)} %get-tuple-element.381), kind=kOutput, calls=%fused_computation.57 | convolution fusion | flops 1208549376 | bytes 20185088 | tf_op jit(solution)/shard_map/while/body/eval_jaxpr/cond/branch_1_fun/transpose(jvp())/dot_general | solution.py:80
  305.1 40.1 %conditional.5 = (bf16[64,1024]{1,0:T(8,128)(2,1)S(1)}) conditional(s32[]{:T(128)} %convert_element_type.246, bf16[64,1024]{1,0:T(8,128)(2,1)S(1)} %bitcast_select_fusion.7, (bf16[64,1024]{1,0:T(8,128)(2,1)S(1)}, bf16[9216,1024]{1,0:T(8,128)(2,1)}, s32[]{:T(128)}, bf16[2,64,1024]{2,1,0:T(8,128)(2,1)S(1)}, f32[2,2048]{1,0:T(2,128)}) %tuple.118), branch_computations={%region_14.14_spmd, %region_15.0_spmd} | conditional | flops 1212638592 | bytes 25697282 | solution.py:139
  312.8 13.2 %fusion.33 = bf16[1,8,8,9216]{3,2,1,0:T(8,128)(2,1)} fusion(bf16[64,1024]{1,0:T(8,128)(2,1)S(1)} %get-tuple-element.380, bf16[9216,1024]{1,0:T(8,128)(2,1)} %get-tuple-element.381), kind=kOutput, calls=%fused_computation.57 | convolution fusion | flops 1208549376 | bytes 20185088 | tf_op jit(solution)/shard_map/while/body/eval_jaxpr/cond/branch_1_fun/transpose(jvp())/dot_general | solution.py:80
  346.9 3.4 collective-permute-done.1
  362.7 3.4 copy.27
  366.1 14.6 %all-reduce.15.cloned.1.call-done = (bf16[2,64,1024]{2,1,0:T(8,128)(2,1)}, bf16[2,64,1024]{2,1,0:T(8,128)(2,1)}) async-done(((bf16[2,64,1024]{2,1,0:T(8,128)(2,1)}, bf16[2,64,1024]{2,1,0:T(8,128)(2,1)}), (bf16[2,64,1024]{2,1,0:T(8,128)(2,1)}, bf16[2,64,1024]{2,1,0:T(8,128)(2,1)})) %all-reduce.15.cloned.1.call-update) | async-done | bytes 524304 | tf_op jit(solution)/shard_map/psum | solution.py:24
  380.8 3.8 multiply_reduce_fusion.5
  384.6 4.9 %psum.39 = bf16[2,2]{0,1:T(2,128)(2,1)S(1)} all-reduce(bf16[2,2]{0,1:T(2,128)(2,1)S(1)} %pad_maximum_fusion.1), channel_id=1, replica_groups=mesh['section'=2,'batch'=16] {'section'}, use_global_device_ids=true, to_apply=%region_32.33 | all-reduce | flops 4 | bytes 16 | tf_op jit(solution)/shard_map/psum | solution.py:101
  (191 shorter events, 129.7 us)
Async XLA Ops:
  8.0 22.7 %copy-start = (bf16[1024,1536]{1,0:T(8,128)(2,1)S(1)}, bf16[1024,1536]{1,0:T(8,128)(2,1)}, u32[]{:S(2)}) copy-start(bf16[1024,1536]{1,0:T(8,128)(2,1)} %param.28) | copy-start | bytes 9437188
  8.0 56.2 %all-reduce.17.cloned.1.call-start = ((), (), s32[]{:S(2)}) async-start(), calls=%async_computation.2 | async-start | bytes 1048576 | tf_op jit(solution)/shard_map/psum | solution.py:101
  12.0 3.4 copy-start.6
  12.0 3.4 copy-start.7
  22.2 3.5 copy-start.8
  25.8 4.8 %copy-start.2 = (f32[2]{0:T(128)}, f32[2]{0:T(128)S(1)}, u32[]{:S(2)}) copy-start(f32[2]{0:T(128)S(1)} %get-tuple-element.477) | copy-start | bytes 28
  25.8 4.8 %copy-start.4 = (f32[2]{0:T(128)}, f32[2]{0:T(128)S(1)}, u32[]{:S(2)}) copy-start(f32[2]{0:T(128)S(1)} %get-tuple-element.479) | copy-start | bytes 28
  32.5 103.8 %all-gather.2.cloned.1.call-start = ((), (), s32[]{:S(2)}) async-start(), calls=%async_computation | async-start | bytes 20054016 | tf_op jit(solution)/shard_map/all_gather | solution.py:165
  33.1 347.6 %all-reduce.15.cloned.1.call-start = ((), (), s32[]{:S(2)}) async-start(), calls=%async_computation.1 | async-start | bytes 1048576 | tf_op jit(solution)/shard_map/psum | solution.py:24
  157.0 5.8 %collective-permute-start = (bf16[64,1024]{1,0:T(8,128)(2,1)S(1)}, bf16[64,1024]{1,0:T(8,128)(2,1)}, u32[]{:S(2)}, u32[]{:S(2)}) collective-permute-start(bf16[64,1024]{1,0:T(8,128)(2,1)S(1)} %get-tuple-element.674), channel_id=1, source_target_pairs={{0,16},{16,0},{1,17},{17,1},{2,18},{18,2},{3,19},{19,3},{4,20},{20... | collective-permute-start | bytes 393224 | tf_op jit(solution)/shard_map/while/body/eval_jaxpr/ppermute | solution.py:19
  182.2 5.1 %collective-permute-start = (bf16[64,1024]{1,0:T(8,128)(2,1)S(1)}, bf16[64,1024]{1,0:T(8,128)(2,1)}, u32[]{:S(2)}, u32[]{:S(2)}) collective-permute-start(bf16[64,1024]{1,0:T(8,128)(2,1)S(1)} %get-tuple-element.674), channel_id=1, source_target_pairs={{0,16},{16,0},{1,17},{17,1},{2,18},{18,2},{3,19},{19,3},{4,20},{20... | collective-permute-start | bytes 393224 | tf_op jit(solution)/shard_map/while/body/eval_jaxpr/ppermute | solution.py:19
  188.3 22.0 %collective-permute-start = (bf16[64,1024]{1,0:T(8,128)(2,1)S(1)}, bf16[64,1024]{1,0:T(8,128)(2,1)}, u32[]{:S(2)}, u32[]{:S(2)}) collective-permute-start(bf16[64,1024]{1,0:T(8,128)(2,1)S(1)} %get-tuple-element.674), channel_id=1, source_target_pairs={{0,16},{16,0},{1,17},{17,1},{2,18},{18,2},{3,19},{19,3},{4,20},{20... | collective-permute-start | bytes 393224 | tf_op jit(solution)/shard_map/while/body/eval_jaxpr/ppermute | solution.py:19
  212.7 45.2 %collective-permute-start.1 = (bf16[64,1024]{1,0:T(8,128)(2,1)S(1)}, bf16[64,1024]{1,0:T(8,128)(2,1)}, u32[]{:S(2)}, u32[]{:S(2)}) collective-permute-start(bf16[64,1024]{1,0:T(8,128)(2,1)S(1)} %get-tuple-element.675), channel_id=1, source_target_pairs={{0,16},{16,0},{1,17},{17,1},{2,18},{18,2},{3,19},{19,3},{4,20},{20... | collective-permute-start | bytes 393224 | tf_op jit(solution)/shard_map/while/body/eval_jaxpr/ppermute | solution.py:19
  264.6 0.5 copy-start.1
  299.0 5.1 %collective-permute-start.1 = (bf16[64,1024]{1,0:T(8,128)(2,1)S(1)}, bf16[64,1024]{1,0:T(8,128)(2,1)}, u32[]{:S(2)}, u32[]{:S(2)}) collective-permute-start(bf16[64,1024]{1,0:T(8,128)(2,1)S(1)} %get-tuple-element.675), channel_id=1, source_target_pairs={{0,16},{16,0},{1,17},{17,1},{2,18},{18,2},{3,19},{19,3},{4,20},{20... | collective-permute-start | bytes 393224 | tf_op jit(solution)/shard_map/while/body/eval_jaxpr/ppermute | solution.py:19
  310.8 0.5 copy-start.1
  345.2 5.1 %collective-permute-start.1 = (bf16[64,1024]{1,0:T(8,128)(2,1)S(1)}, bf16[64,1024]{1,0:T(8,128)(2,1)}, u32[]{:S(2)}, u32[]{:S(2)}) collective-permute-start(bf16[64,1024]{1,0:T(8,128)(2,1)S(1)} %get-tuple-element.675), channel_id=1, source_target_pairs={{0,16},{16,0},{1,17},{17,1},{2,18},{18,2},{3,19},{19,3},{4,20},{20... | collective-permute-start | bytes 393224 | tf_op jit(solution)/shard_map/while/body/eval_jaxpr/ppermute | solution.py:19
  362.7 18.0 %copy-start.3 = (f32[2]{0:T(128)S(1)}, f32[2]{0:T(128)}, u32[]{:S(2)}) copy-start(f32[2]{0:T(128)} %copy-done.2) | copy-start | bytes 28
  380.8 9.4 %copy-start.5 = (f32[2]{0:T(128)S(1)}, f32[2]{0:T(128)}, u32[]{:S(2)}) copy-start(f32[2]{0:T(128)} %copy-done.4) | copy-start | bytes 28
Sparse Core Ops, SparseCore 0:
  32.7 31.5 all-reduce.16
  352.9 27.8 all-reduce.14
Sparse Core Ops, SparseCore 1:
  34.7 101.6 all-gather.1

commit v2 on v1

v2 whole, which is shorter than its diff:
```python
import math

import jax
import jax.numpy as jnp
from jax import lax
from jax.experimental import pallas as pl
from jax.experimental.pallas import tpu as pltpu
from jax.sharding import PartitionSpec as P

CH = 1024
GROUPS = 32
TEMB = 1024
GRID = 8
TSTEPS = 1000
PV = 3072


def noise_levels(timestep):
    beta_rates = jnp.linspace(0.0001, 0.02, TSTEPS, dtype=jnp.float32)
    steps = jnp.arange(TSTEPS, dtype=jnp.int32)[None, :]
    return jnp.prod(jnp.where(steps <= timestep[:, None], 1.0 - beta_rates[None, :], 1.0), axis=1)


def time_features(timestep):
    half_width = TEMB // 2
    frequency = jnp.exp(-math.log(10000.0) * jnp.arange(half_width, dtype=jnp.float32) / half_width)
    angles = timestep.astype(jnp.float32)[:, None] * frequency[None, :]
    return jax.nn.silu(jnp.concatenate([jnp.cos(angles), jnp.sin(angles)], axis=1)).astype(
        jnp.bfloat16
    )


CELLS = GRID * GRID


def circulants(hue_angle, saturation):
    cosine = jnp.cos(hue_angle)
    sine_of = jnp.sin(hue_angle) / math.sqrt(3.0)
    turning = (cosine * (2.0 / 3.0), -cosine / 3.0 - sine_of, -cosine / 3.0 + sine_of)
    matrix = tuple(1.0 / 3.0 + saturation * entry for entry in turning)
    sine_whole = jnp.sin(hue_angle)
    cos_part = cosine / math.sqrt(3.0)
    slope = (
        -sine_whole * (2.0 / 3.0),
        sine_whole / 3.0 - cos_part,
        sine_whole / 3.0 + cos_part,
    )
    return matrix, tuple(saturation * entry for entry in slope), turning


def turned(pixels):
    colour = lax.broadcasted_iota(jnp.int32, (1, 1, pixels.shape[2]), 2) % 3
    after = jnp.where(colour < 2, jnp.roll(pixels, -1, 2), jnp.roll(pixels, 2, 2))
    before = jnp.where(colour > 0, jnp.roll(pixels, 1, 2), jnp.roll(pixels, -2, 2))
    return after, before


def group_mean(total):
    channels = total.shape[1]
    width = channels // GROUPS
    total = jnp.broadcast_to(total, (8, channels))
    lane = lax.broadcasted_iota(jnp.int32, (8, channels), 1)
    step = 1
    while step < width:
        total = total + jnp.where(
            (lane & step) != 0,
            pltpu.roll(total, step, 1),
            pltpu.roll(total, channels - step, 1),
        )
        step *= 2
    return total[0:1] * (1.0 / (CELLS * width))


def normalised(value):
    centred = value - group_mean(jnp.sum(value, axis=0, keepdims=True))
    spread_sq = group_mean(jnp.sum(centred * centred, axis=0, keepdims=True))
    inverse = lax.rsqrt(spread_sq + 1e-05)
    return centred * inverse, inverse


def activate(feature_ref, scaling_ref, act_ref):
    channels = feature_ref.shape[1]
    for image in range(feature_ref.shape[0] // CELLS):
        rows = pl.ds(image * CELLS, CELLS)
        normed, _ = normalised(feature_ref[rows, :].astype(jnp.float32))
        pre = normed * (1.0 + scaling_ref[image : image + 1, :channels])
        pre = pre + scaling_ref[image : image + 1, channels:]
        act_ref[rows, :] = pre * jax.nn.sigmoid(pre)


def branch_back(feature_ref, scaling_ref, image, slope_in):
    channels = feature_ref.shape[1]
    rows = pl.ds(image * CELLS, CELLS)
    normed, inverse = normalised(feature_ref[rows, :].astype(jnp.float32))
    gain = 1.0 + scaling_ref[image : image + 1, :channels]
    pre = normed * gain + scaling_ref[image : image + 1, channels:]
    gate = jax.nn.sigmoid(pre)
    slope = slope_in * (gate * (1.0 + pre * (1.0 - gate))) * gain
    mean_slope = group_mean(jnp.sum(slope, axis=0, keepdims=True))
    mean_cross = group_mean(jnp.sum(slope * normed, axis=0, keepdims=True))
    return inverse * (slope - mean_slope - normed * mean_cross)


def neighbours(values, down, right):
    rows = values.shape[0]
    offset = GRID * down + right
    shifted = pltpu.roll(values, lax.rem(2 * rows - offset, rows), 0)
    row = lax.broadcasted_iota(jnp.int32, (rows, 1), 0)
    high = (row // GRID) % GRID + down
    wide = row % GRID + right
    inside = (high >= 0) & (high < GRID) & (wide >= 0) & (wide < GRID)
    return jnp.where(inside, shifted, 0.0).astype(jnp.bfloat16)


def forward_kernel(feature_ref, scaling_ref, weight_ref, out_ref, act_ref, total_ref):
    tap = pl.program_id(0)

    @pl.when(tap == 0)
    def _():
        activate(feature_ref, scaling_ref, act_ref)
        total_ref[...] = feature_ref[...].astype(jnp.float32)

    columns = neighbours(act_ref[...], tap // 3 - 1, tap % 3 - 1)
    total_ref[...] += jnp.dot(columns, weight_ref[...], preferred_element_type=jnp.float32)

    @pl.when(tap == 8)
    def _():
        out_ref[...] = total_ref[...].astype(jnp.bfloat16)


def add_transposed(tap, upstream_ref, weight_ref, total_ref):
    @pl.when(tap == 0)
    def _():
        total_ref[...] = jnp.zeros_like(total_ref)

    columns = neighbours(upstream_ref[...].astype(jnp.float32), 1 - tap // 3, 1 - tap % 3)
    total_ref[...] += lax.dot_general(
        columns, weight_ref[...], (((1,), (1,)), ((), ())), preferred_element_type=jnp.float32
    )


def transposed_kernel(upstream_ref, weight_ref, out_ref, total_ref):
    tap = pl.program_id(0)
    add_transposed(tap, upstream_ref, weight_ref, total_ref)

    @pl.when(tap == 8)
    def _():
        out_ref[...] = total_ref[...].astype(jnp.bfloat16)


def finish_back(upstream_ref, feature_ref, scaling_ref, slope_ref, out_ref):
    for image in range(upstream_ref.shape[0] // CELLS):
        rows = pl.ds(image * CELLS, CELLS)
        slope_in = slope_ref[rows, :].astype(jnp.bfloat16).astype(jnp.float32)
        grad = branch_back(feature_ref, scaling_ref, image, slope_in)
        out_ref[rows, :] = (upstream_ref[rows, :].astype(jnp.float32) + grad).astype(jnp.bfloat16)


def adjoint_kernel(upstream_ref, feature_ref, scaling_ref, weight_ref, out_ref, total_ref):
    tap = pl.program_id(0)
    add_transposed(tap, upstream_ref, weight_ref, total_ref)

    @pl.when(tap == 8)
    def _():
        finish_back(upstream_ref, feature_ref, scaling_ref, total_ref, out_ref)


def whole(shape):
    return pl.BlockSpec(shape, lambda tap: (0, 0))


def by_tap(kernel, small, weight, scratch):
    rows, channels = small[0].shape
    return pl.pallas_call(
        kernel,
        grid=(9,),
        in_specs=[whole(value.shape) for value in small]
        + [pl.BlockSpec((channels, channels), lambda tap: (tap, 0))],
        out_specs=whole((rows, channels)),
        out_shape=jax.ShapeDtypeStruct((rows, channels), jnp.bfloat16),
        scratch_shapes=[pltpu.VMEM((rows, channels), jnp.float32)] * scratch,
        compiler_params=pltpu.CompilerParams(vmem_limit_bytes=24 * 1024 * 1024),
        cost_estimate=pl.CostEstimate(
            flops=2 * rows * weight.size,
            bytes_accessed=2 * weight.size,
            transcendentals=rows * channels,
        ),
    )(*small, weight)


def forward_block(feature, scaling, weight):
    return by_tap(forward_kernel, (feature, scaling), weight, 2)


def transposed_conv(upstream, weight):
    return by_tap(transposed_kernel, (upstream,), weight, 1)


def adjoint_block(upstream, feature, scaling, weight):
    return by_tap(adjoint_kernel, (upstream, feature, scaling), weight, 1)


def adjoint_from(upstream, feature, scaling, slope_in):
    return pl.pallas_call(
        finish_back,
        out_shape=jax.ShapeDtypeStruct(upstream.shape, jnp.bfloat16),
    )(upstream, feature, scaling, slope_in)


def moved(value, steps):
    count = lax.axis_size("section")
    return lax.ppermute(value, "section", [(at, (at + steps) % count) for at in range(count)])


def section_sum(value):
    if lax.axis_size("section") == 2:
        return value.astype(jnp.float32) + moved(value, 1).astype(jnp.float32)
    return lax.psum(value, "section").astype(jnp.float32)


def two_sections(first, seed, scaling, weight):
    place = lax.axis_index("section")
    early = lax.cond(
        place == 0,
        lambda: forward_block(first, scaling, weight),
        lambda: transposed_conv(seed, weight),
    )
    arrived = moved(early, 1)
    back = moved(adjoint_from(seed, arrived, scaling, early), 1)
    late = lax.cond(
        place == 0,
        lambda: adjoint_block(back, first, scaling, weight),
        lambda: forward_block(arrived, scaling, weight),
    )
    final = jnp.where(place == 0, moved(late, 1), late)
    return final, late


def many_sections(first, seed, scaling, weight):
    sections = lax.axis_size("section")
    place = lax.axis_index("section")
    entering, final = first, first
    current = first
    for at in range(sections):
        entering = jnp.where(place == at, current, entering)
        result = forward_block(current, scaling, weight)
        final = jnp.where(place == at, result, final)
        current = moved(result, 1)
    final = lax.psum(jnp.where(place == sections - 1, final, jnp.zeros_like(final)), "section")
    current = seed
    last = seed
    for at in reversed(range(sections)):
        last = adjoint_block(current, entering, scaling, weight)
        current = moved(last, -1)
    return final, last


def local(
    images,
    noise_draw,
    cotangent,
    hue_angle,
    saturation,
    timestep,
    stem_weight,
    conv_weight,
    emb_weight,
    head_weight,
):
    sections = lax.axis_size("section")
    place = lax.axis_index("section")
    number = images.shape[0]
    columns_here = images.shape[2]
    rows = number * CELLS
    full_conv = lax.all_gather(conv_weight[0], "batch", axis=0, tiled=True)
    level = noise_levels(timestep)
    root_level = jnp.sqrt(level)[:, None, None]
    root_noise = jnp.sqrt(1.0 - level)[:, None, None]
    matrix, hue_slope, sat_slope = circulants(hue_angle, saturation)
    after, before = turned(images)
    variants = [images, after, before]
    wide = [variant.astype(jnp.float32) for variant in variants]
    coloured = sum(entry[:, None, None] * variant for entry, variant in zip(matrix, wide))
    noised = root_level * coloured + root_noise * noise_draw.astype(jnp.float32)
    weighted = cotangent.astype(jnp.float32) * (1.0 / math.sqrt(CELLS * PV))
    eps_grad = (-(root_noise / root_level) * weighted).astype(jnp.bfloat16)
    entry_part = jnp.dot(
        noised.astype(jnp.bfloat16).reshape(rows, columns_here),
        stem_weight,
        preferred_element_type=jnp.float32,
    )
    seed_part = lax.dot_general(
        eps_grad.reshape(rows, columns_here),
        head_weight,
        (((1,), (1,)), ((), ())),
        preferred_element_type=jnp.float32,
    )
    ends = section_sum(jnp.stack([entry_part, seed_part]).astype(jnp.bfloat16))
    ends = ends.astype(jnp.bfloat16)
    scaling = jnp.dot(time_features(timestep), emb_weight[0], preferred_element_type=jnp.float32)
    probes = jnp.dot(
        jnp.stack(variants).reshape(3 * rows, columns_here),
        stem_weight,
        preferred_element_type=jnp.float32,
    )
    probes = section_sum(probes.astype(jnp.bfloat16)).reshape(3, number, CELLS, CH)
    direct = jnp.stack([jnp.sum(weighted * variant, axis=(1, 2)) for variant in wide])
    run = two_sections if sections == 2 else many_sections
    final, adjoint = run(ends[0], ends[1], scaling, full_conv)
    adjoint = adjoint.astype(jnp.float32).reshape(1, number, CELLS, CH)
    through = jnp.sum(adjoint * probes, axis=(2, 3)) * root_level[None, :, 0, 0]
    sums = direct + jnp.where(place == 0, through, 0.0)
    parts = jnp.stack(
        [sum(entry * one for entry, one in zip(slope, sums)) for slope in (hue_slope, sat_slope)],
        axis=1,
    )
    predicted = jnp.dot(final, head_weight, preferred_element_type=jnp.float32)
    predicted = predicted.reshape(number, CELLS, columns_here)
    purified = ((noised - root_noise * predicted) / root_level).astype(jnp.bfloat16)
    return (purified, section_sum(parts))


def solution(mesh):
    in_specs = (
        P("batch", None, "section"),
        P("batch", None, "section"),
        P("batch", None, "section"),
        P("batch"),
        P("batch"),
        P("batch"),
        P("section", None),
        P("section", "batch", None),
        P("section", None, None),
        P(None, "section"),
    )
    out_specs = (P("batch", None, "section"), P("batch", None))
    return jax.shard_map(local, mesh=mesh, in_specs=in_specs, out_specs=out_specs, check_vma=False)
```

time: 403 us -> 180 us (0.45)
  local copies, waits for them, and re-layouts: 72.3 us -> 5.74 us
  starting transfers between devices: 63.8 us -> 8.99 us
  matrix products: 61.1 us -> 9.47 us
  other arithmetic: 52.4 us -> 11.5 us
  waiting for transfers between devices: 130 us -> 97.2 us
  Pallas kernels: 0 us -> 31.6 us
  blocking collectives: 4.94 us -> 0 us
    ppermute x6, starting transfers between devices: 63.7 us -> 8.95 us  [moved(): lax.ppermute(value, 'section', [(at, (at + steps) % count) for at in rang...]
    dot_general x8 -> x4, matrix products: 57.6 us -> 6.6 us  [the longest x1 2.54 us: local(): predicted = jnp.dot(final, head_weight, preferred_element_type=jnp.float32)]
    psum x2 -> x0, waiting for transfers between devices: 42 us -> none  [the longest x1 27.4 us: section_total(): lax.psum(partial_sum.astype(jnp.bfloat16), 'section').astype(jnp.float32)]
    pallas_call x0 -> x3, Pallas kernels: none -> 31.6 us  [the longest x2 28.1 us: by_tap(): pl.pallas_call(kernel, grid=(9,), in_specs=[whole(value.shape) for value...]
    reduce_sum x19 -> x1, local copies, waits for them, and re-layouts: 29.2 us -> 0.08 us  [local(): through = jnp.sum(adjoint * probes, axis=(2, 3)) * root_level[None, :, 0, 0]]
    reduce_sum x27 -> x3, other arithmetic: 25.3 us -> 3.21 us  [the longest x2 1.82 us: local(): through = jnp.sum(adjoint * probes, axis=(2, 3)) * root_level[None, :, 0, 0]]
    mul x14 -> x0, local copies, waits for them, and re-layouts: 15.2 us -> none  [the longest x2 6.42 us: apply_map(): matrix[:, None, None, :, :] * pixels[:, :, :, None, :]]
    ppermute x6, waiting for transfers between devices: 15.1 us -> 22.9 us  [moved(): lax.ppermute(value, 'section', [(at, (at + steps) % count) for at in rang...]
  transfers between devices with their start and end apart: 9 -> 7, of which waited for: 9 -> 5; matrix products, arithmetic and copies ran while one was open for 7% -> 13% of each run, Pallas kernels for 0% -> 18%
where the time goes in v2:
time: 180 us; the launch traced here: 179 us
  waiting for transfers between devices  97.2 us (54%)
  Pallas kernels  31.6 us (18%)
  between operations  14.3 us (8%)
  other arithmetic  11.5 us (6%)
  matrix products  9.47 us (5%)
  starting transfers between devices  8.99 us (5%)
  local copies, waits for them, and re-layouts  5.74 us (3%)
    all_gather x1, waiting for transfers between devices, local(): full_conv = lax.all_gather(conv_weight[0], 'batch', axis=0, tiled=True)  73.6 us
    pallas_call x2, Pallas kernels, by_tap(): pl.pallas_call(kernel, grid=(9,), in_specs=[whole(value.shape) for value...  28.1 us
    ppermute x6, waiting for transfers between devices, moved(): lax.ppermute(value, 'section', [(at, (at + steps) % count) for at in rang...  22.9 us
    ppermute x6, starting transfers between devices, moved(): lax.ppermute(value, 'section', [(at, (at + steps) % count) for at in rang...  8.95 us
  transfers between devices with their start and end apart: 7, of which 5 were waited for; matrix products, arithmetic and copies ran while one was open for 13% of the time, Pallas kernels for 18%

profile of v2, /device:TPU:0, one launch (start us, length us, event | category | flops | bytes accessed | tf_op | source)
XLA Modules:
  0.0 178.9 jit_solution(12055565577814194131)
XLA Ops:
  12.1 1.3 slice_bitcast_fusion.8
  13.7 1.4 fusion.12
  15.3 1.1 fusion.4
  16.5 1.6 fusion.40
  19.7 3.0 %collective-permute-start = (bf16[2,128,1024]{2,1,0:T(8,128)(2,1)}, bf16[2,128,1024]{2,1,0:T(8,128)(2,1)}, u32[]{:S(2)}, u32[]{:S(2)}) collective-permute-start(bf16[2,128,1024]{2,1,0:T(8,128)(2,1)} %pad_maximum_fusion.1), channel_id=1, source_target_pairs={{0,16},{16,0},{1,17},{17,1},{2,18},{18,2},{3,19},{19,3},{4,20},{20... | collective-permute-start | bytes 1572872 | tf_op jit(solution)/shard_map/ppermute | solution.py:212
  23.3 2.3 %convolution_convert_fusion = bf16[384,1024]{1,0:T(8,128)(2,1)} fusion(bf16[384,1536]{1,0:T(8,128)(2,1)S(1)} %bitcast.91, bf16[1536,1024]{1,0:T(8,128)(2,1)S(1)} %copy-done), kind=kOutput, calls=%fused_computation.4 | convolution fusion | flops 1208352768 | bytes 5111808 | tf_op jit(solution)/shard_map/dot_general | solution.py:301
  25.8 2.9 %fusion.scaling_ref = f32[2,2048]{1,0:T(2,128)S(1)} fusion(bf16[1,1024,2048]{2,1,0:T(8,128)(2,1)} %param.22, f32[2,512]{1,0:T(2,128)S(1)} %get-tuple-element.77, f32[2,512]{1,0:T(2,128)S(1)} %get-tuple-element.76), kind=kOutput, calls=%fused_computation | convolution fusion | flops 8400896 | bytes 4218880 | tf_op jit(solution)/shard_map/dot_general | solution.py:300
  28.7 7.0 %collective-permute-done = bf16[2,128,1024]{2,1,0:T(8,128)(2,1)} collective-permute-done((bf16[2,128,1024]{2,1,0:T(8,128)(2,1)}, bf16[2,128,1024]{2,1,0:T(8,128)(2,1)}, u32[]{:S(2)}, u32[]{:S(2)}) %collective-permute-start) | collective-permute-done | bytes 524320 | tf_op jit(solution)/shard_map/ppermute | solution.py:212
  35.7 1.2 add_convert_fusion
  37.7 73.6 %all-gather.3.cloned.1.call-done = bf16[1,9216,1024]{2,1,0:T(8,128)(2,1)} async-done(((bf16[1,576,1024]{2,1,0:T(8,128)(2,1)}), bf16[1,9216,1024]{2,1,0:T(8,128)(2,1)}) %all-gather.3.cloned.1.call-update) | async-done | bytes 18874384 | tf_op jit(solution)/shard_map/all_gather | solution.py:275
  111.3 12.9 %conditional.2 = (bf16[128,1024]{1,0:T(8,128)(2,1)}) conditional(s32[]{:T(128)} %convert_element_type.58, (bf16[128,1024]{1,0:T(8,128)(2,1)}, bf16[9216,1024]{1,0:T(8,128)(2,1)}) %tuple.59, (bf16[128,1024]{1,0:T(8,128)(2,1)S(1)}, f32[2,2048]{1,0:T(2,128)S(1)}, bf16[9216,1024]{1,0:T(8,128)(2,1)}) %tuple.60), branch_computations={%region_1.2_spmd, %region_2.3_spmd} | conditional | flops 2415919104 | bytes 18874376 | solution.py:223
  111.3 12.9 %branch_1_fun.2 = bf16[128,1024]{1,0:T(8,128)(2,1)} custom-call(bf16[128,1024]{1,0:T(8,128)(2,1)S(1)} %get-tuple-element.32.feature_ref, f32[2,2048]{1,0:T(2,128)S(1)} %get-tuple-element.33.scaling_ref, bf16[9216,1024]{1,0:T(8,128)(2,1)} %get-tuple-element.34.weight_ref), custom_call_target="tpu_custom_call" | custom-call | flops 2415919104 | bytes 18874368 | tf_op jit(solution)/shard_map/cond/branch_1_fun/pallas_call | solution.py:174
  124.2 2.1 %collective-permute-start.1 = (bf16[128,1024]{1,0:T(8,128)(2,1)}, bf16[128,1024]{1,0:T(8,128)(2,1)}, u32[]{:S(2)}, u32[]{:S(2)}) collective-permute-start(bf16[128,1024]{1,0:T(8,128)(2,1)} %get-tuple-element.88.slope_ref), channel_id=1, source_target_pairs={{0,16},{16,0},{1,17},{17,1},{2,18},{18,2},{3,19},{19,3},{4,20},{20... | collective-permute-start | bytes 786440 | tf_op jit(solution)/shard_map/ppermute | solution.py:212
  126.3 7.0 %collective-permute-done.1.feature_ref = bf16[128,1024]{1,0:T(8,128)(2,1)} collective-permute-done((bf16[128,1024]{1,0:T(8,128)(2,1)}, bf16[128,1024]{1,0:T(8,128)(2,1)}, u32[]{:S(2)}, u32[]{:S(2)}) %collective-permute-start.1) | collective-permute-done | bytes 262176 | tf_op jit(solution)/shard_map/ppermute | solution.py:212
  133.4 3.5 %shard_map.113 = bf16[128,1024]{1,0:T(8,128)(2,1)} custom-call(bf16[128,1024]{1,0:T(8,128)(2,1)} %get-tuple-element.56.upstream_ref, bf16[128,1024]{1,0:T(8,128)(2,1)} %collective-permute-done.1.feature_ref, f32[2,2048]{1,0:T(2,128)S(1)} %fusion.scaling_ref, bf16[128,1024]{1,0:T(8,128)(2,1)} %get-tuple-element.88.slope_ref), custom_call_target="tpu_custom_call" | custom-call | tf_op jit(solution)/shard_map/pallas_call | solution.py:204
  136.9 1.7 collective-permute-start.2
  138.6 6.5 %collective-permute-done.2 = bf16[128,1024]{1,0:T(8,128)(2,1)} collective-permute-done((bf16[128,1024]{1,0:T(8,128)(2,1)}, bf16[128,1024]{1,0:T(8,128)(2,1)}, u32[]{:S(2)}, u32[]{:S(2)}) %collective-permute-start.2) | collective-permute-done | bytes 262176 | tf_op jit(solution)/shard_map/ppermute | solution.py:212
  145.2 15.4 %conditional.3 = (bf16[128,1024]{1,0:T(8,128)(2,1)}) conditional(s32[]{:T(128)} %convert_element_type.58, (bf16[128,1024]{1,0:T(8,128)(2,1)}, f32[2,2048]{1,0:T(2,128)S(1)}, bf16[9216,1024]{1,0:T(8,128)(2,1)}) %tuple.61, (bf16[128,1024]{1,0:T(8,128)(2,1)}, bf16[128,1024]{1,0:T(8,128)(2,1)S(1)}, f32[2,2048]{1,0:T(2,128)S(1)}, ...), branch_computations={%region_3.4_spmd, %region_4.5_spmd} | conditional | flops 2415919104 | bytes 18874376 | solution.py:230
  145.4 15.2 %branch_1_fun.3 = bf16[128,1024]{1,0:T(8,128)(2,1)} custom-call(bf16[128,1024]{1,0:T(8,128)(2,1)} %get-tuple-element.38.upstream_ref, bf16[128,1024]{1,0:T(8,128)(2,1)S(1)} %get-tuple-element.39.feature_ref, f32[2,2048]{1,0:T(2,128)S(1)} %get-tuple-element.40.scaling_ref, bf16[9216,1024]{1,0:T(8,128)(2,1)} %get-tuple-element.41.weight_ref), custom_call_target="tpu_custom_call" | custom-call | flops 2415919104 | bytes 18874368 | tf_op jit(solution)/shard_map/cond/branch_1_fun/pallas_call | solution.py:174
  160.6 1.0 bitcast_convert_fusion
  161.6 1.7 fusion.2
  163.6 2.1 %collective-permute-start.5 = (f32[2,2]{0,1:T(2,128)S(1)}, f32[2,2]{0,1:T(2,128)S(1)}, u32[]{:S(2)}, u32[]{:S(2)}) collective-permute-start(f32[2,2]{0,1:T(2,128)S(1)} %pad_maximum_fusion.3), channel_id=1, source_target_pairs={{0,16},{16,0},{1,17},{17,1},{2,18},{18,2},{3,19},{19,3},{4,20},{20... | collective-permute-start | bytes 56 | tf_op jit(solution)/shard_map/ppermute | solution.py:212
  165.7 2.2 %collective-permute-done.5 = f32[2,2]{0,1:T(2,128)S(1)} collective-permute-done((f32[2,2]{0,1:T(2,128)S(1)}, f32[2,2]{0,1:T(2,128)S(1)}, u32[]{:S(2)}, u32[]{:S(2)}) %collective-permute-start.5) | collective-permute-done | bytes 48 | tf_op jit(solution)/shard_map/ppermute | solution.py:212
  168.6 2.5 %fusion.16 = f32[128,1536]{1,0:T(8,128)S(1)} fusion(bf16[1024,1536]{1,0:T(8,128)(2,1)} %param.23, bf16[128,1024]{1,0:T(8,128)(2,1)S(1)} %collective-permute-done.3, bf16[128,1024]{1,0:T(8,128)(2,1)} %get-tuple-element.89, pred[]{:T(512)S(6)} %eq.4), kind=kOutput, calls=%fused_computation.35 | convolution fusion | flops 402784256 | bytes 4456449 | tf_op jit(solution)/shard_map/dot_general | solution.py:317
  (67 shorter events, 10.2 us)
Async XLA Ops:
  7.2 11.0 %copy-start = (bf16[1536,1024]{1,0:T(8,128)(2,1)S(1)}, bf16[1536,1024]{1,0:T(8,128)(2,1)}, u32[]{:S(2)}) copy-start(bf16[1536,1024]{1,0:T(8,128)(2,1)} %param.20) | copy-start | bytes 9437188
  7.2 6.3 %copy-start.1 = (bf16[2,64,1536]{2,1,0:T(8,128)(2,1)S(1)}, bf16[2,64,1536]{2,1,0:T(8,128)(2,1)}, u32[]{:S(2)}) copy-start(bf16[2,64,1536]{2,1,0:T(8,128)(2,1)} %param.14) | copy-start | bytes 1179652
  7.2 104.1 %all-gather.3.cloned.1.call-start = ((), (), s32[]{:S(2)}) async-start(), calls=%async_computation | async-start | bytes 20054016 | tf_op jit(solution)/shard_map/all_gather | solution.py:275
  7.9 5.8 %copy-start.8 = (bf16[2,64,1536]{2,1,0:T(8,128)(2,1)S(1)}, bf16[2,64,1536]{2,1,0:T(8,128)(2,1)}, u32[]{:S(2)}) copy-start(bf16[2,64,1536]{2,1,0:T(8,128)(2,1)} %param.16) | copy-start | bytes 1179652
  9.7 5.4 %copy-start.12 = (f32[2]{0:T(128)}, f32[2]{0:T(128)S(1)}, u32[]{:S(2)}) copy-start(f32[2]{0:T(128)S(1)} %get-tuple-element.84) | copy-start | bytes 28
  9.7 5.4 %copy-start.14 = (f32[2]{0:T(128)}, f32[2]{0:T(128)S(1)}, u32[]{:S(2)}) copy-start(f32[2]{0:T(128)S(1)} %get-tuple-element.85) | copy-start | bytes 28
  13.4 1.9 %copy-start.2 = (bf16[1024,1536]{1,0:T(8,128)(2,1)S(1)}, bf16[1024,1536]{1,0:T(8,128)(2,1)}, u32[]{:S(2)}) copy-start(bf16[1024,1536]{1,0:T(8,128)(2,1)} %param.23) | copy-start | bytes 9437188
  13.7 2.8 %copy-start.9 = (bf16[2,64,1536]{2,1,0:T(8,128)(2,1)S(1)}, bf16[2,64,1536]{2,1,0:T(8,128)(2,1)}, u32[]{:S(2)}) copy-start(bf16[2,64,1536]{2,1,0:T(8,128)(2,1)} %param.15) | copy-start | bytes 1179652
  16.5 2.2 %copy-start.4 = (bf16[1,128,1024]{2,1,0:T(8,128)(2,1)}, bf16[1,128,1024]{2,1,0:T(8,128)(2,1)S(1)}, u32[]{:S(2)}) copy-start(bf16[1,128,1024]{2,1,0:T(8,128)(2,1)S(1)} %fusion.4) | copy-start | bytes 786436
  18.7 0.9 copy-start.6
  19.7 16.0 %collective-permute-start = (bf16[2,128,1024]{2,1,0:T(8,128)(2,1)}, bf16[2,128,1024]{2,1,0:T(8,128)(2,1)}, u32[]{:S(2)}, u32[]{:S(2)}) collective-permute-start(bf16[2,128,1024]{2,1,0:T(8,128)(2,1)} %pad_maximum_fusion.1), channel_id=1, source_target_pairs={{0,16},{16,0},{1,17},{17,1},{2,18},{18,2},{3,19},{19,3},{4,20},{20... | collective-permute-start | bytes 1572872 | tf_op jit(solution)/shard_map/ppermute | solution.py:212
  23.2 2.4 %copy-start.16 = (s32[2]{0:T(128)S(1)}, s32[2]{0:T(128)}, u32[]{:S(2)}) copy-start(s32[2]{0:T(128)} %param.19) | copy-start | bytes 28
  25.6 10.1 %copy-start.5 = (bf16[1,128,1024]{2,1,0:T(8,128)(2,1)S(1)}, bf16[1,128,1024]{2,1,0:T(8,128)(2,1)}, u32[]{:S(2)}) copy-start(bf16[1,128,1024]{2,1,0:T(8,128)(2,1)} %copy-done.4) | copy-start | bytes 786436
  25.6 136.0 %collective-permute-start.4 = (bf16[384,1024]{1,0:T(8,128)(2,1)}, bf16[384,1024]{1,0:T(8,128)(2,1)}, u32[]{:S(2)}, u32[]{:S(2)}) collective-permute-start(bf16[384,1024]{1,0:T(8,128)(2,1)} %convolution_convert_fusion), channel_id=1, source_target_pairs={{0,16},{16,0},{1,17},{17,1},{2,18},{18,2},{3,19},{19,3},{4,20},{20... | collective-permute-start | bytes 2359304 | tf_op jit(solution)/shard_map/ppermute | solution.py:212
  25.6 10.1 %copy-start.7 = (bf16[1,128,1024]{2,1,0:T(8,128)(2,1)S(1)}, bf16[1,128,1024]{2,1,0:T(8,128)(2,1)}, u32[]{:S(2)}) copy-start(bf16[1,128,1024]{2,1,0:T(8,128)(2,1)} %copy-done.6) | copy-start | bytes 786436
  124.2 9.2 %collective-permute-start.1 = (bf16[128,1024]{1,0:T(8,128)(2,1)}, bf16[128,1024]{1,0:T(8,128)(2,1)}, u32[]{:S(2)}, u32[]{:S(2)}) collective-permute-start(bf16[128,1024]{1,0:T(8,128)(2,1)} %get-tuple-element.88.slope_ref), channel_id=1, source_target_pairs={{0,16},{16,0},{1,17},{17,1},{2,18},{18,2},{3,19},{19,3},{4,20},{20... | collective-permute-start | bytes 786440 | tf_op jit(solution)/shard_map/ppermute | solution.py:212
  136.9 8.3 %collective-permute-start.2 = (bf16[128,1024]{1,0:T(8,128)(2,1)}, bf16[128,1024]{1,0:T(8,128)(2,1)}, u32[]{:S(2)}, u32[]{:S(2)}) collective-permute-start(bf16[128,1024]{1,0:T(8,128)(2,1)} %shard_map.113), channel_id=1, source_target_pairs={{0,16},{16,0},{1,17},{17,1},{2,18},{18,2},{3,19},{19,3},{4,20},{20... | collective-permute-start | bytes 786440 | tf_op jit(solution)/shard_map/ppermute | solution.py:212
  145.1 18.4 %copy-start.10 = (f32[2]{0:T(128)S(1)}, f32[2]{0:T(128)}, u32[]{:S(2)}) copy-start(f32[2]{0:T(128)} %get-tuple-element.52) | copy-start | bytes 28
  145.1 18.4 %copy-start.11 = (f32[2]{0:T(128)S(1)}, f32[2]{0:T(128)}, u32[]{:S(2)}) copy-start(f32[2]{0:T(128)} %param.18) | copy-start | bytes 28
  145.2 18.4 %copy-start.13 = (f32[2]{0:T(128)S(1)}, f32[2]{0:T(128)}, u32[]{:S(2)}) copy-start(f32[2]{0:T(128)} %copy-done.12) | copy-start | bytes 28
  145.2 18.4 %copy-start.15 = (f32[2]{0:T(128)S(1)}, f32[2]{0:T(128)}, u32[]{:S(2)}) copy-start(f32[2]{0:T(128)} %copy-done.14) | copy-start | bytes 28
  160.6 8.0 %collective-permute-start.3 = (bf16[128,1024]{1,0:T(8,128)(2,1)}, bf16[128,1024]{1,0:T(8,128)(2,1)S(1)}, u32[]{:S(2)}, u32[]{:S(2)}) collective-permute-start(bf16[128,1024]{1,0:T(8,128)(2,1)} %get-tuple-element.89), channel_id=1, source_target_pairs={{0,16},{16,0},{1,17},{17,1},{2,18},{18,2},{3,19},{19,3},{4,20},{20... | collective-permute-start | bytes 786440 | tf_op jit(solution)/shard_map/ppermute | solution.py:212
  163.6 4.3 %collective-permute-start.5 = (f32[2,2]{0,1:T(2,128)S(1)}, f32[2,2]{0,1:T(2,128)S(1)}, u32[]{:S(2)}, u32[]{:S(2)}) collective-permute-start(f32[2,2]{0,1:T(2,128)S(1)} %pad_maximum_fusion.3), channel_id=1, source_target_pairs={{0,16},{16,0},{1,17},{17,1},{2,18},{18,2},{3,19},{19,3},{4,20},{20... | collective-permute-start | bytes 56 | tf_op jit(solution)/shard_map/ppermute | solution.py:212
  168.6 2.6 %copy-start.3 = (f32[2,64,1536]{2,1,0:T(8,128)S(1)}, f32[2,64,1536]{2,1,0:T(8,128)}, u32[]{:S(2)}) copy-start(f32[2,64,1536]{2,1,0:T(8,128)} %get-tuple-element.54) | copy-start | bytes 2359300
Sparse Core Ops, SparseCore 0:
  9.6 101.6 all-gather.2

commit v3 on v2

--- a/solution.py
+++ b/solution.py
@@ -1,3 +1,4 @@
+import functools
 import math
 
 import jax
@@ -112,40 +113,68 @@
     return jnp.where(inside, shifted, 0.0).astype(jnp.bfloat16)
 
 
-def forward_kernel(feature_ref, scaling_ref, weight_ref, out_ref, act_ref, total_ref):
-    tap = pl.program_id(0)
-
-    @pl.when(tap == 0)
+TAPS = 3
+
+
+def column_slices(weight_refs, begin=0):
+    for ref in weight_refs:
+        yield ref, pl.ds(begin, ref.shape[1])
+        begin += ref.shape[1]
+
+
+def add_forward(step, begin, act_ref, weight_refs, total_ref):
+    channels = act_ref.shape[1]
+    values = act_ref[...]
+    for right in range(TAPS):
+        columns = neighbours(values, step - 1, right - 1)
+        taken = pl.ds(right * channels, channels)
+        for ref, here in column_slices(weight_refs):
+            total_ref[:, here] += jnp.dot(
+                columns, ref[taken, :], preferred_element_type=jnp.float32
+            )
+
+
+def forward_kernel(begin, feature_ref, scaling_ref, *refs):
+    *weight_refs, out_ref, act_ref, total_ref = refs
+    step = pl.program_id(0)
+
+    @pl.when(step == 0)
     def _():
         activate(feature_ref, scaling_ref, act_ref)
-        total_ref[...] = feature_ref[...].astype(jnp.float32)
-
-    columns = neighbours(act_ref[...], tap // 3 - 1, tap % 3 - 1)
-    total_ref[...] += jnp.dot(columns, weight_ref[...], preferred_element_type=jnp.float32)
-
-    @pl.when(tap == 8)
+        here = pl.ds(begin, total_ref.shape[1])
+        total_ref[...] = feature_ref[:, here].astype(jnp.float32)
+
+    add_forward(step, begin, act_ref, weight_refs, total_ref)
+
+    @pl.when(step == TAPS - 1)
     def _():
         out_ref[...] = total_ref[...].astype(jnp.bfloat16)
 
 
-def add_transposed(tap, upstream_ref, weight_ref, total_ref):
-    @pl.when(tap == 0)
-    def _():
-        total_ref[...] = jnp.zeros_like(total_ref)
-
-    columns = neighbours(upstream_ref[...].astype(jnp.float32), 1 - tap // 3, 1 - tap % 3)
-    total_ref[...] += lax.dot_general(
-        columns, weight_ref[...], (((1,), (1,)), ((), ())), preferred_element_type=jnp.float32
-    )
-
-
-def transposed_kernel(upstream_ref, weight_ref, out_ref, total_ref):
-    tap = pl.program_id(0)
-    add_transposed(tap, upstream_ref, weight_ref, total_ref)
-
-    @pl.when(tap == 8)
-    def _():
-        out_ref[...] = total_ref[...].astype(jnp.bfloat16)
+def add_transposed(step, begin, upstream_ref, weight_refs, total_ref):
+    channels = upstream_ref.shape[1]
+    values = upstream_ref[...].astype(jnp.float32)
+    for right in range(TAPS):
+        taken = pl.ds(right * channels, channels)
+        for ref, here in column_slices(weight_refs, begin):
+            columns = neighbours(values[:, here.start : here.start + here.size], 1 - step, 1 - right)
+            total_ref[...] += lax.dot_general(
+                columns,
+                ref[taken, :],
+                (((1,), (1,)), ((), ())),
+                preferred_element_type=jnp.float32,
+            )
+
+
+def transposed_kernel(begin, upstream_ref, before_ref, *refs):
+    *weight_refs, total_ref = refs
+    step = pl.program_id(0)
+
+    @pl.when(step == 0)
+    def _():
+        total_ref[...] = before_ref[...]
+
+    add_transposed(step, begin, upstream_ref, weight_refs, total_ref)
 
 
 def finish_back(upstream_ref, feature_ref, scaling_ref, slope_ref, out_ref):
@@ -156,48 +185,62 @@
         out_ref[rows, :] = (upstream_ref[rows, :].astype(jnp.float32) + grad).astype(jnp.bfloat16)
 
 
-def adjoint_kernel(upstream_ref, feature_ref, scaling_ref, weight_ref, out_ref, total_ref):
-    tap = pl.program_id(0)
-    add_transposed(tap, upstream_ref, weight_ref, total_ref)
-
-    @pl.when(tap == 8)
+def adjoint_kernel(upstream_ref, feature_ref, scaling_ref, *refs):
+    *weight_refs, out_ref, total_ref = refs
+    step = pl.program_id(0)
+
+    @pl.when(step == 0)
+    def _():
+        total_ref[...] = jnp.zeros_like(total_ref)
+
+    add_transposed(step, 0, upstream_ref, weight_refs, total_ref)
+
+    @pl.when(step == TAPS - 1)
     def _():
         finish_back(upstream_ref, feature_ref, scaling_ref, total_ref, out_ref)
 
 
 def whole(shape):
-    return pl.BlockSpec(shape, lambda tap: (0, 0))
-
-
-def by_tap(kernel, small, weight, scratch):
+    return pl.BlockSpec(shape, lambda step: (0, 0))
+
+
+def by_tap(kernel, small, weights, width, kind, scratch):
     rows, channels = small[0].shape
+    size = sum(weight.size for weight in weights)
     return pl.pallas_call(
         kernel,
-        grid=(9,),
+        grid=(TAPS,),
         in_specs=[whole(value.shape) for value in small]
-        + [pl.BlockSpec((channels, channels), lambda tap: (tap, 0))],
-        out_specs=whole((rows, channels)),
-        out_shape=jax.ShapeDtypeStruct((rows, channels), jnp.bfloat16),
-        scratch_shapes=[pltpu.VMEM((rows, channels), jnp.float32)] * scratch,
-        compiler_params=pltpu.CompilerParams(vmem_limit_bytes=24 * 1024 * 1024),
+        + [
+            pl.BlockSpec((TAPS * channels, weight.shape[1]), lambda step: (step, 0))
+            for weight in weights
+        ],
+        out_specs=whole((rows, width)),
+        out_shape=jax.ShapeDtypeStruct((rows, width), kind),
+        scratch_shapes=[pltpu.VMEM((rows, across), jnp.float32) for across in scratch],
+        compiler_params=pltpu.CompilerParams(vmem_limit_bytes=32 * 1024 * 1024),
         cost_estimate=pl.CostEstimate(
-            flops=2 * rows * weight.size,
-            bytes_accessed=2 * weight.size,
-            transcendentals=rows * channels,
+            flops=2 * rows * size, bytes_accessed=2 * size, transcendentals=rows * channels
         ),
-    )(*small, weight)
-
-
-def forward_block(feature, scaling, weight):
-    return by_tap(forward_kernel, (feature, scaling), weight, 2)
-
-
-def transposed_conv(upstream, weight):
-    return by_tap(transposed_kernel, (upstream,), weight, 1)
-
-
-def adjoint_block(upstream, feature, scaling, weight):
-    return by_tap(adjoint_kernel, (upstream, feature, scaling), weight, 1)
+    )(*small, *weights)
+
+
+def forward_block(feature, scaling, weights, begin=0):
+    width = sum(weight.shape[1] for weight in weights)
+    kernel = functools.partial(forward_kernel, begin)
+    scratch = (feature.shape[1], width)
+    return by_tap(kernel, (feature, scaling), weights, width, jnp.bfloat16, scratch)
+
+
+def transposed_conv(upstream, before, weights, begin):
+    kernel = functools.partial(transposed_kernel, begin)
+    return by_tap(kernel, (upstream, before), weights, upstream.shape[1], jnp.float32, ())
+
+
+def adjoint_block(upstream, feature, scaling, weights):
+    width = upstream.shape[1]
+    small = (upstream, feature, scaling)
+    return by_tap(adjoint_kernel, small, weights, width, jnp.bfloat16, (width,))
 
 
 def adjoint_from(upstream, feature, scaling, slope_in):
@@ -218,39 +261,49 @@
     return lax.psum(value, "section").astype(jnp.float32)
 
 
-def two_sections(first, seed, scaling, weight):
+def two_sections(first, seed, scaling, weights):
     place = lax.axis_index("section")
-    early = lax.cond(
-        place == 0,
-        lambda: forward_block(first, scaling, weight),
-        lambda: transposed_conv(seed, weight),
-    )
-    arrived = moved(early, 1)
-    back = moved(adjoint_from(seed, arrived, scaling, early), 1)
+    pieces = []
+    slope = jnp.zeros(seed.shape, jnp.float32)
+    begin = 0
+    for part in weights:
+
+        def ahead(part=part, slope=slope, begin=begin):
+            return forward_block(first, scaling, (part,), begin), slope
+
+        def behind(part=part, slope=slope, begin=begin):
+            other = jnp.zeros((seed.shape[0], part.shape[1]), jnp.bfloat16)
+            return other, transposed_conv(seed, slope, (part,), begin)
+
+        piece, slope = lax.cond(place == 0, ahead, behind)
+        pieces.append(moved(piece, 1))
+        begin += part.shape[1]
+    arrived = jnp.concatenate(pieces, axis=1)
+    back = moved(adjoint_from(seed, arrived, scaling, slope), 1)
     late = lax.cond(
         place == 0,
-        lambda: adjoint_block(back, first, scaling, weight),
-        lambda: forward_block(arrived, scaling, weight),
+        lambda: adjoint_block(back, first, scaling, weights),
+        lambda: forward_block(arrived, scaling, weights),
     )
     final = jnp.where(place == 0, moved(late, 1), late)
     return final, late
 
 
-def many_sections(first, seed, scaling, weight):
+def many_sections(first, seed, scaling, weights):
     sections = lax.axis_size("section")
     place = lax.axis_index("section")
     entering, final = first, first
     current = first
     for at in range(sections):
         entering = jnp.where(place == at, current, entering)
-        result = forward_block(current, scaling, weight)
+        result = forward_block(current, scaling, weights)
         final = jnp.where(place == at, result, final)
         current = moved(result, 1)
     final = lax.psum(jnp.where(place == sections - 1, final, jnp.zeros_like(final)), "section")
     current = seed
     last = seed
     for at in reversed(range(sections)):
-        last = adjoint_block(current, entering, scaling, weight)
+        last = adjoint_block(current, entering, scaling, weights)
         current = moved(last, -1)
     return final, last
 
@@ -272,7 +325,11 @@
     number = images.shape[0]
     columns_here = images.shape[2]
     rows = number * CELLS
-    full_conv = lax.all_gather(conv_weight[0], "batch", axis=0, tiled=True)
+    half = CH // 2
+    full_conv = tuple(
+        lax.all_gather(conv_weight[0, :, begin : begin + half], "batch", axis=0, tiled=True)
+        for begin in (0, half)
+    )
     level = noise_levels(timestep)
     root_level = jnp.sqrt(level)[:, None, None]
     root_noise = jnp.sqrt(1.0 - level)[:, None, None]

time: 180 us -> 234 us (1.30)
  waiting for transfers between devices: 97.2 us -> 145 us
  local copies, waits for them, and re-layouts: 5.74 us -> 9.95 us
  starting transfers between devices: 8.99 us -> 12.1 us
  other arithmetic: 11.5 us -> 13.9 us
    all_gather x1 -> x2, waiting for transfers between devices: 73.6 us -> 125 us  [local(): lax.all_gather(conv_weight[0, :, begin:begin + half], 'batch', axis=0, ti...]
    ppermute x6 -> x7, waiting for transfers between devices: 22.9 us -> 18.7 us  [moved(): lax.ppermute(value, 'section', [(at, (at + steps) % count) for at in rang...]
    ppermute x6 -> x7, starting transfers between devices: 8.95 us -> 12 us  [moved(): lax.ppermute(value, 'section', [(at, (at + steps) % count) for at in rang...]
    slice x0 -> x1, local copies, waits for them, and re-layouts: none -> 2.54 us  [local(): conv_weight[0, :, begin:begin + half]]
    pallas_call x2 -> x3, Pallas kernels: 28.1 us -> 26.2 us  [by_tap(): pl.pallas_call(kernel, grid=(TAPS,), in_specs=[whole(value.shape) for val...]
  transfers between devices with their start and end apart: 7 -> 9, of which waited for: 5 -> 6; matrix products, arithmetic and copies ran while one was open for 13% -> 11% of each run, Pallas kernels for 18% -> 13%
where the time goes in v3:
time: 234 us
  waiting for transfers between devices  145 us (62%)
  Pallas kernels  29.8 us (13%)
  between operations  14.4 us (6%)
  other arithmetic  13.9 us (6%)
  starting transfers between devices  12.1 us (5%)
  local copies, waits for them, and re-layouts  9.95 us (4%)
  matrix products  8.53 us (4%)
    all_gather x2, waiting for transfers between devices, local(): lax.all_gather(conv_weight[0, :, begin:begin + half], 'batch', axis=0, ti...  125 us
    pallas_call x3, Pallas kernels, by_tap(): pl.pallas_call(kernel, grid=(TAPS,), in_specs=[whole(value.shape) for val...  26.2 us
    ppermute x7, waiting for transfers between devices, moved(): lax.ppermute(value, 'section', [(at, (at + steps) % count) for at in rang...  18.7 us
    ppermute x7, starting transfers between devices, moved(): lax.ppermute(value, 'section', [(at, (at + steps) % count) for at in rang...  12 us
  transfers between devices with their start and end apart: 9, of which 6 were waited for; matrix products, arithmetic and copies ran while one was open for 11% of the time, Pallas kernels for 13%

profile of v3, /device:TPU:0, one launch (start us, length us, event | category | flops | bytes accessed | tf_op | source)
XLA Modules:
  0.0 233.6 jit_solution(11680354364810326790)
XLA Ops:
  7.3 2.5 %fusion.42 = (bf16[1,576,512]{2,1,0:T(8,128)(2,1)}, bf16[1,576,512]{2,1,0:T(8,128)(2,1)}) fusion(bf16[1,576,1024]{2,1,0:T(8,128)(2,1)} %param.23), kind=kLoop, calls=%fused_computation.97 | loop fusion | bytes 2359296 | tf_op jit(solution)/shard_map/slice | solution.py:330
  16.6 1.6 fusion.40
  20.9 3.0 %collective-permute-start = (bf16[2,128,1024]{2,1,0:T(8,128)(2,1)}, bf16[2,128,1024]{2,1,0:T(8,128)(2,1)}, u32[]{:S(2)}, u32[]{:S(2)}) collective-permute-start(bf16[2,128,1024]{2,1,0:T(8,128)(2,1)} %pad_maximum_fusion.1), channel_id=1, source_target_pairs={{0,16},{16,0},{1,17},{17,1},{2,18},{18,2},{3,19},{19,3},{4,20},{20... | collective-permute-start | bytes 1572872 | tf_op jit(solution)/shard_map/ppermute | solution.py:255
  24.5 2.1 maximum_select_fusion.2
  28.6 7.6 %collective-permute-done = bf16[2,128,1024]{2,1,0:T(8,128)(2,1)} collective-permute-done((bf16[2,128,1024]{2,1,0:T(8,128)(2,1)}, bf16[2,128,1024]{2,1,0:T(8,128)(2,1)}, u32[]{:S(2)}, u32[]{:S(2)}) %collective-permute-start) | collective-permute-done | bytes 524320 | tf_op jit(solution)/shard_map/ppermute | solution.py:255
  38.1 56.4 %all-gather.5.cloned.1.call-done = bf16[1,9216,512]{2,1,0:T(8,128)(2,1)} async-done(((bf16[1,576,512]{2,1,0:T(8,128)(2,1)}), bf16[1,9216,512]{2,1,0:T(8,128)(2,1)}) %all-gather.5.cloned.1.call-update) | async-done | bytes 9437200 | tf_op jit(solution)/shard_map/all_gather | solution.py:330
  94.5 7.2 %conditional.3 = (bf16[128,512]{1,0:T(8,128)(2,1)}, f32[128,1024]{1,0:T(8,128)S(1)}) conditional(s32[]{:T(128)} %convert_element_type.59, (bf16[128,1024]{1,0:T(8,128)(2,1)}, bf16[9216,512]{1,0:T(8,128)(2,1)}) %tuple.76, (bf16[128,1024]{1,0:T(8,128)(2,1)S(1)}, f32[2,2048]{1,0:T(2,128)S(1)}, bf16[9216,512]{1,0:T(8,128)(2,1)}) %tuple.77), branch_computations={%region_1.2_spmd, %region_2.3_spmd} | conditional | flops 1207959552 | bytes 10092566 | solution.py:278
  94.5 7.2 %branch_1_fun.3 = bf16[128,512]{1,0:T(8,128)(2,1)} custom-call(bf16[128,1024]{1,0:T(8,128)(2,1)S(1)} %get-tuple-element.47.feature_ref, f32[2,2048]{1,0:T(2,128)S(1)} %get-tuple-element.48.scaling_ref, bf16[9216,512]{1,0:T(8,128)(2,1)} %get-tuple-element.49.refs_0_), custom_call_target="tpu_custom_call" | custom-call | flops 1207959552 | bytes 9437184 | tf_op jit(solution)/shard_map/cond/branch_1_fun/pallas_call | solution.py:210
  102.9 3.6 %convolution_convert_fusion = bf16[384,1024]{1,0:T(8,128)(2,1)} fusion(bf16[384,1536]{1,0:T(8,128)(2,1)} %bitcast.96, bf16[1536,1024]{1,0:T(8,128)(2,1)S(1)} %copy-done), kind=kOutput, calls=%fused_computation.4 | convolution fusion | flops 1208352768 | bytes 5111808 | tf_op jit(solution)/shard_map/dot_general | solution.py:358
  107.5 68.9 %all-gather.7.cloned.1.call-done = bf16[1,9216,512]{2,1,0:T(8,128)(2,1)} async-done(((bf16[1,576,512]{2,1,0:T(8,128)(2,1)}), bf16[1,9216,512]{2,1,0:T(8,128)(2,1)}) %all-gather.7.cloned.1.call-update) | async-done | bytes 9437200 | tf_op jit(solution)/shard_map/all_gather | solution.py:330
  176.4 6.7 %conditional.4 = (bf16[128,512]{1,0:T(8,128)(2,1)S(1)}, f32[128,1024]{1,0:T(8,128)}) conditional(s32[]{:T(128)} %convert_element_type.59, (bf16[128,1024]{1,0:T(8,128)(2,1)}, f32[128,1024]{1,0:T(8,128)}, bf16[9216,512]{1,0:T(8,128)(2,1)}) %tuple.84, (bf16[128,1024]{1,0:T(8,128)(2,1)S(1)}, f32[2,2048]{1,0:T(2,128)S(1)}, bf16[9216,512]{1,0:T(8,128)(2,1)}, ...), branch_computations={%region_3.4_spmd, %region_4.5_spmd} | conditional | flops 1207959552 | bytes 10616850 | solution.py:278
  176.4 6.5 %branch_1_fun.4 = bf16[128,512]{1,0:T(8,128)(2,1)S(1)} custom-call(bf16[128,1024]{1,0:T(8,128)(2,1)S(1)} %get-tuple-element.53.feature_ref, f32[2,2048]{1,0:T(2,128)S(1)} %get-tuple-element.54.scaling_ref, bf16[9216,512]{1,0:T(8,128)(2,1)} %get-tuple-element.55.refs_0_), custom_call_target="tpu_custom_call" | custom-call | flops 1207959552 | bytes 9437184 | tf_op jit(solution)/shard_map/cond/branch_1_fun/pallas_call | solution.py:210
  183.1 3.1 %collective-permute-start.2 = (bf16[128,512]{1,0:T(8,128)(2,1)S(1)}, bf16[128,512]{1,0:T(8,128)(2,1)S(1)}, u32[]{:S(2)}, u32[]{:S(2)}) collective-permute-start(bf16[128,512]{1,0:T(8,128)(2,1)S(1)} %get-tuple-element.74), channel_id=1, source_target_pairs={{0,16},{16,0},{1,17},{17,1},{2,18},{18,2},{3,19},{19,3},{4,20},{20... | collective-permute-start | bytes 393224 | tf_op jit(solution)/shard_map/ppermute | solution.py:255
  186.2 1.6 constant_dynamic-update-slice_fusion.1
  187.8 2.3 collective-permute-done.2
  190.8 3.6 %shard_map.113 = bf16[128,1024]{1,0:T(8,128)(2,1)} custom-call(bf16[128,1024]{1,0:T(8,128)(2,1)} %get-tuple-element.90.upstream_ref, bf16[128,1024]{1,0:T(8,128)(2,1)} %constant_dynamic-update-slice_fusion.feature_ref, f32[2,2048]{1,0:T(2,128)S(1)} %fusion.scaling_ref, f32[128,1024]{1,0:T(8,128)} %get-tuple-element.75.slope_ref), custom_call_target="tpu_custom_call" | custom-call | tf_op jit(solution)/shard_map/pallas_call | solution.py:247
  194.4 1.7 collective-permute-start.3
  196.1 6.6 %collective-permute-done.3 = bf16[128,1024]{1,0:T(8,128)(2,1)} collective-permute-done((bf16[128,1024]{1,0:T(8,128)(2,1)}, bf16[128,1024]{1,0:T(8,128)(2,1)}, u32[]{:S(2)}, u32[]{:S(2)}) %collective-permute-start.3) | collective-permute-done | bytes 262176 | tf_op jit(solution)/shard_map/ppermute | solution.py:255
  202.7 12.5 %conditional.5 = (bf16[128,1024]{1,0:T(8,128)(2,1)}) conditional(s32[]{:T(128)} %convert_element_type.59, (bf16[128,1024]{1,0:T(8,128)(2,1)}, f32[2,2048]{1,0:T(2,128)S(1)}, bf16[9216,512]{1,0:T(8,128)(2,1)}, bf16[9216,512]{1,0:T(8,128)(2,1)}) %tuple.82, (bf16[128,1024]{1,0:T(8,128)(2,1)}, bf16[128,1024]{1,0:T(8,128)(2,1)S(1)}, ...), branch_computations={%region_5.6_spmd, %region_6.7_spmd} | conditional | flops 2415919104 | bytes 18874376 | solution.py:283
  202.7 12.5 %branch_1_fun.5 = bf16[128,1024]{1,0:T(8,128)(2,1)} custom-call(bf16[128,1024]{1,0:T(8,128)(2,1)} %get-tuple-element.61.upstream_ref, bf16[128,1024]{1,0:T(8,128)(2,1)S(1)} %get-tuple-element.62.feature_ref, f32[2,2048]{1,0:T(2,128)S(1)} %get-tuple-element.63.scaling_ref, bf16[9216,512]{1,0:T(8,128)(2,1)} %get-tuple-element.64.refs_0_, ...), custom_call_target="tpu_custom_call" | custom-call | flops 2415919104 | bytes 18874368 | tf_op jit(solution)/shard_map/cond/branch_1_fun/pallas_call | solution.py:210
  216.3 1.7 fusion.2
  218.3 2.1 collective-permute-start.6
  220.3 2.2 collective-permute-done.6
  223.3 2.5 %fusion.16 = f32[128,1536]{1,0:T(8,128)S(1)} fusion(bf16[1024,1536]{1,0:T(8,128)(2,1)} %param.25, bf16[128,1024]{1,0:T(8,128)(2,1)S(1)} %collective-permute-done.4, bf16[128,1024]{1,0:T(8,128)(2,1)} %get-tuple-element.130, pred[]{:T(512)S(6)} %eq.4), kind=kOutput, calls=%fused_computation.35 | convolution fusion | flops 402784256 | bytes 4456449 | tf_op jit(solution)/shard_map/dot_general | solution.py:374
  (92 shorter events, 19.7 us)
Async XLA Ops:
  7.2 11.1 %copy-start = (bf16[1536,1024]{1,0:T(8,128)(2,1)S(1)}, bf16[1536,1024]{1,0:T(8,128)(2,1)}, u32[]{:S(2)}) copy-start(bf16[1536,1024]{1,0:T(8,128)(2,1)} %param.22) | copy-start | bytes 9437188
  7.2 3.5 %copy-start.20 = (s32[2]{0:T(128)S(1)}, s32[2]{0:T(128)}, u32[]{:S(2)}) copy-start(s32[2]{0:T(128)} %param.21) | copy-start | bytes 28
  7.2 3.7 %copy-start.23 = (f32[2]{0:T(128)S(1)}, f32[2]{0:T(128)}, u32[]{:S(2)}) copy-start(f32[2]{0:T(128)} %param.19) | copy-start | bytes 28
  7.2 4.5 %copy-start.1 = (bf16[2,64,1536]{2,1,0:T(8,128)(2,1)S(1)}, bf16[2,64,1536]{2,1,0:T(8,128)(2,1)}, u32[]{:S(2)}) copy-start(bf16[2,64,1536]{2,1,0:T(8,128)(2,1)} %param.16) | copy-start | bytes 1179652
  7.2 87.3 %all-gather.5.cloned.1.call-start = ((), (), s32[]{:S(2)}) async-start(), calls=%async_computation | async-start | bytes 10027008 | tf_op jit(solution)/shard_map/all_gather | solution.py:330
  9.8 166.6 %all-gather.7.cloned.1.call-start = ((), (), s32[]{:S(2)}) async-start(), calls=%async_computation.1 | async-start | bytes 10027008 | tf_op jit(solution)/shard_map/all_gather | solution.py:330
  10.6 4.6 %copy-start.10 = (bf16[2,64,1536]{2,1,0:T(8,128)(2,1)S(1)}, bf16[2,64,1536]{2,1,0:T(8,128)(2,1)}, u32[]{:S(2)}) copy-start(bf16[2,64,1536]{2,1,0:T(8,128)(2,1)} %param.18) | copy-start | bytes 1179652
  18.9 5.1 %copy-start.21 = (s32[2]{0:T(128)S(1)}, s32[2]{0:T(128)}, u32[]{:S(2)}) copy-start(s32[2]{0:T(128)} %param.21) | copy-start | bytes 28
  20.9 15.2 %collective-permute-start = (bf16[2,128,1024]{2,1,0:T(8,128)(2,1)}, bf16[2,128,1024]{2,1,0:T(8,128)(2,1)}, u32[]{:S(2)}, u32[]{:S(2)}) collective-permute-start(bf16[2,128,1024]{2,1,0:T(8,128)(2,1)} %pad_maximum_fusion.1), channel_id=1, source_target_pairs={{0,16},{16,0},{1,17},{17,1},{2,18},{18,2},{3,19},{19,3},{4,20},{20... | collective-permute-start | bytes 1572872 | tf_op jit(solution)/shard_map/ppermute | solution.py:255
  26.6 9.6 %copy-start.7 = (bf16[1,128,1024]{2,1,0:T(8,128)(2,1)S(1)}, bf16[1,128,1024]{2,1,0:T(8,128)(2,1)}, u32[]{:S(2)}) copy-start(bf16[1,128,1024]{2,1,0:T(8,128)(2,1)} %copy-done.6) | copy-start | bytes 786436
  26.6 9.6 %copy-start.9 = (bf16[1,128,1024]{2,1,0:T(8,128)(2,1)S(1)}, bf16[1,128,1024]{2,1,0:T(8,128)(2,1)}, u32[]{:S(2)}) copy-start(bf16[1,128,1024]{2,1,0:T(8,128)(2,1)} %copy-done.8) | copy-start | bytes 786436
  101.7 4.8 %copy-start.3 = (f32[128,1024]{1,0:T(8,128)}, f32[128,1024]{1,0:T(8,128)S(1)}, u32[]{:S(2)}) copy-start(f32[128,1024]{1,0:T(8,128)S(1)} %get-tuple-element.73) | copy-start | bytes 1572868
  101.7 84.4 %collective-permute-start.1 = (bf16[128,512]{1,0:T(8,128)(2,1)}, bf16[128,512]{1,0:T(8,128)(2,1)}, u32[]{:S(2)}, u32[]{:S(2)}) collective-permute-start(bf16[128,512]{1,0:T(8,128)(2,1)} %get-tuple-element.72), channel_id=1, source_target_pairs={{0,16},{16,0},{1,17},{17,1},{2,18},{18,2},{3,19},{19,3},{4,20},{20... | collective-permute-start | bytes 393224 | tf_op jit(solution)/shard_map/ppermute | solution.py:255
  106.5 109.8 %collective-permute-start.5 = (bf16[384,1024]{1,0:T(8,128)(2,1)}, bf16[384,1024]{1,0:T(8,128)(2,1)}, u32[]{:S(2)}, u32[]{:S(2)}) collective-permute-start(bf16[384,1024]{1,0:T(8,128)(2,1)} %convolution_convert_fusion), channel_id=1, source_target_pairs={{0,16},{16,0},{1,17},{17,1},{2,18},{18,2},{3,19},{19,3},{4,20},{20... | collective-permute-start | bytes 2359304 | tf_op jit(solution)/shard_map/ppermute | solution.py:255
  183.1 7.0 %collective-permute-start.2 = (bf16[128,512]{1,0:T(8,128)(2,1)S(1)}, bf16[128,512]{1,0:T(8,128)(2,1)S(1)}, u32[]{:S(2)}, u32[]{:S(2)}) collective-permute-start(bf16[128,512]{1,0:T(8,128)(2,1)S(1)} %get-tuple-element.74), channel_id=1, source_target_pairs={{0,16},{16,0},{1,17},{17,1},{2,18},{18,2},{3,19},{19,3},{4,20},{20... | collective-permute-start | bytes 393224 | tf_op jit(solution)/shard_map/ppermute | solution.py:255
  194.4 8.3 %collective-permute-start.3 = (bf16[128,1024]{1,0:T(8,128)(2,1)}, bf16[128,1024]{1,0:T(8,128)(2,1)}, u32[]{:S(2)}, u32[]{:S(2)}) collective-permute-start(bf16[128,1024]{1,0:T(8,128)(2,1)} %shard_map.113), channel_id=1, source_target_pairs={{0,16},{16,0},{1,17},{17,1},{2,18},{18,2},{3,19},{19,3},{4,20},{20... | collective-permute-start | bytes 786440 | tf_op jit(solution)/shard_map/ppermute | solution.py:255
  202.7 15.5 %copy-start.12 = (f32[2]{0:T(128)S(1)}, f32[2]{0:T(128)}, u32[]{:S(2)}) copy-start(f32[2]{0:T(128)} %get-tuple-element.82) | copy-start | bytes 28
  202.7 15.5 %copy-start.13 = (f32[2]{0:T(128)S(1)}, f32[2]{0:T(128)}, u32[]{:S(2)}) copy-start(f32[2]{0:T(128)} %get-tuple-element.83) | copy-start | bytes 28
  202.7 15.5 %copy-start.14 = (f32[2]{0:T(128)S(1)}, f32[2]{0:T(128)}, u32[]{:S(2)}) copy-start(f32[2]{0:T(128)} %get-tuple-element.84) | copy-start | bytes 28
  202.7 15.5 %copy-start.15 = (f32[2]{0:T(128)S(1)}, f32[2]{0:T(128)}, u32[]{:S(2)}) copy-start(f32[2]{0:T(128)} %param.20) | copy-start | bytes 28
  202.7 15.5 %copy-start.17 = (f32[2]{0:T(128)S(1)}, f32[2]{0:T(128)}, u32[]{:S(2)}) copy-start(f32[2]{0:T(128)} %copy-done.16) | copy-start | bytes 28
  202.7 15.5 %copy-start.19 = (f32[2]{0:T(128)S(1)}, f32[2]{0:T(128)}, u32[]{:S(2)}) copy-start(f32[2]{0:T(128)} %copy-done.18) | copy-start | bytes 28
  215.2 8.0 %collective-permute-start.4 = (bf16[128,1024]{1,0:T(8,128)(2,1)}, bf16[128,1024]{1,0:T(8,128)(2,1)S(1)}, u32[]{:S(2)}, u32[]{:S(2)}) collective-permute-start(bf16[128,1024]{1,0:T(8,128)(2,1)} %get-tuple-element.130), channel_id=1, source_target_pairs={{0,16},{16,0},{1,17},{17,1},{2,18},{18,2},{3,19},{19,3},{4,20},{20... | collective-permute-start | bytes 786440 | tf_op jit(solution)/shard_map/ppermute | solution.py:255
  218.3 4.3 %collective-permute-start.6 = (f32[2,2]{0,1:T(2,128)S(1)}, f32[2,2]{0,1:T(2,128)S(1)}, u32[]{:S(2)}, u32[]{:S(2)}) collective-permute-start(f32[2,2]{0,1:T(2,128)S(1)} %pad_maximum_fusion.3), channel_id=1, source_target_pairs={{0,16},{16,0},{1,17},{17,1},{2,18},{18,2},{3,19},{19,3},{4,20},{20... | collective-permute-start | bytes 56 | tf_op jit(solution)/shard_map/ppermute | solution.py:255
  (9 other events, 18.9 us)
Sparse Core Ops, SparseCore 0:
  10.3 84.1 all-gather.4
  96.8 79.5 all-gather.6

commit v4 on v3

--- a/solution.py
+++ b/solution.py
@@ -1,4 +1,3 @@
-import functools
 import math
 
 import jax
@@ -116,13 +115,14 @@
 TAPS = 3
 
 
-def column_slices(weight_refs, begin=0):
+def column_slices(weight_refs):
+    begin = 0
     for ref in weight_refs:
         yield ref, pl.ds(begin, ref.shape[1])
         begin += ref.shape[1]
 
 
-def add_forward(step, begin, act_ref, weight_refs, total_ref):
+def add_forward(step, act_ref, weight_refs, total_ref):
     channels = act_ref.shape[1]
     values = act_ref[...]
     for right in range(TAPS):
@@ -134,29 +134,28 @@
             )
 
 
-def forward_kernel(begin, feature_ref, scaling_ref, *refs):
+def forward_kernel(feature_ref, scaling_ref, *refs):
     *weight_refs, out_ref, act_ref, total_ref = refs
     step = pl.program_id(0)
 
     @pl.when(step == 0)
     def _():
         activate(feature_ref, scaling_ref, act_ref)
-        here = pl.ds(begin, total_ref.shape[1])
-        total_ref[...] = feature_ref[:, here].astype(jnp.float32)
-
-    add_forward(step, begin, act_ref, weight_refs, total_ref)
+        total_ref[...] = feature_ref[...].astype(jnp.float32)
+
+    add_forward(step, act_ref, weight_refs, total_ref)
 
     @pl.when(step == TAPS - 1)
     def _():
         out_ref[...] = total_ref[...].astype(jnp.bfloat16)
 
 
-def add_transposed(step, begin, upstream_ref, weight_refs, total_ref):
+def add_transposed(step, upstream_ref, weight_refs, total_ref):
     channels = upstream_ref.shape[1]
     values = upstream_ref[...].astype(jnp.float32)
     for right in range(TAPS):
         taken = pl.ds(right * channels, channels)
-        for ref, here in column_slices(weight_refs, begin):
+        for ref, here in column_slices(weight_refs):
             columns = neighbours(values[:, here.start : here.start + here.size], 1 - step, 1 - right)
             total_ref[...] += lax.dot_general(
                 columns,
@@ -166,15 +165,19 @@
             )
 
 
-def transposed_kernel(begin, upstream_ref, before_ref, *refs):
-    *weight_refs, total_ref = refs
+def transposed_kernel(upstream_ref, *refs):
+    *weight_refs, out_ref, total_ref = refs
     step = pl.program_id(0)
 
     @pl.when(step == 0)
     def _():
-        total_ref[...] = before_ref[...]
-
-    add_transposed(step, begin, upstream_ref, weight_refs, total_ref)
+        total_ref[...] = jnp.zeros_like(total_ref)
+
+    add_transposed(step, upstream_ref, weight_refs, total_ref)
+
+    @pl.when(step == TAPS - 1)
+    def _():
+        out_ref[...] = total_ref[...].astype(jnp.bfloat16)
 
 
 def finish_back(upstream_ref, feature_ref, scaling_ref, slope_ref, out_ref):
@@ -193,7 +196,7 @@
     def _():
         total_ref[...] = jnp.zeros_like(total_ref)
 
-    add_transposed(step, 0, upstream_ref, weight_refs, total_ref)
+    add_transposed(step, upstream_ref, weight_refs, total_ref)
 
     @pl.when(step == TAPS - 1)
     def _():
@@ -225,16 +228,14 @@
     )(*small, *weights)
 
 
-def forward_block(feature, scaling, weights, begin=0):
-    width = sum(weight.shape[1] for weight in weights)
-    kernel = functools.partial(forward_kernel, begin)
-    scratch = (feature.shape[1], width)
-    return by_tap(kernel, (feature, scaling), weights, width, jnp.bfloat16, scratch)
-
-
-def transposed_conv(upstream, before, weights, begin):
-    kernel = functools.partial(transposed_kernel, begin)
-    return by_tap(kernel, (upstream, before), weights, upstream.shape[1], jnp.float32, ())
+def forward_block(feature, scaling, weights):
+    width = feature.shape[1]
+    return by_tap(forward_kernel, (feature, scaling), weights, width, jnp.bfloat16, (width, width))
+
+
+def transposed_conv(upstream, weights):
+    width = upstream.shape[1]
+    return by_tap(transposed_kernel, (upstream,), weights, width, jnp.bfloat16, (width,))
 
 
 def adjoint_block(upstream, feature, scaling, weights):
@@ -263,23 +264,13 @@
 
 def two_sections(first, seed, scaling, weights):
     place = lax.axis_index("section")
-    pieces = []
-    slope = jnp.zeros(seed.shape, jnp.float32)
-    begin = 0
-    for part in weights:
-
-        def ahead(part=part, slope=slope, begin=begin):
-            return forward_block(first, scaling, (part,), begin), slope
-
-        def behind(part=part, slope=slope, begin=begin):
-            other = jnp.zeros((seed.shape[0], part.shape[1]), jnp.bfloat16)
-            return other, transposed_conv(seed, slope, (part,), begin)
-
-        piece, slope = lax.cond(place == 0, ahead, behind)
-        pieces.append(moved(piece, 1))
-        begin += part.shape[1]
-    arrived = jnp.concatenate(pieces, axis=1)
-    back = moved(adjoint_from(seed, arrived, scaling, slope), 1)
+    early = lax.cond(
+        place == 0,
+        lambda: forward_block(first, scaling, weights),
+        lambda: transposed_conv(seed, weights),
+    )
+    arrived = moved(early, 1)
+    back = moved(adjoint_from(seed, arrived, scaling, early), 1)
     late = lax.cond(
         place == 0,
         lambda: adjoint_block(back, first, scaling, weights),
@@ -325,11 +316,7 @@
     number = images.shape[0]
     columns_here = images.shape[2]
     rows = number * CELLS
-    half = CH // 2
-    full_conv = tuple(
-        lax.all_gather(conv_weight[0, :, begin : begin + half], "batch", axis=0, tiled=True)
-        for begin in (0, half)
-    )
+    full_conv = (lax.all_gather(conv_weight[0], "batch", axis=0, tiled=True),)
     level = noise_levels(timestep)
     root_level = jnp.sqrt(level)[:, None, None]
     root_noise = jnp.sqrt(1.0 - level)[:, None, None]

time: 234 us -> 174 us (0.74)
  waiting for transfers between devices: 145 us -> 97.2 us
  local copies, waits for them, and re-layouts: 9.95 us -> 5.74 us
  Pallas kernels: 29.8 us -> 25.9 us
  starting transfers between devices: 12.1 us -> 9.17 us
  other arithmetic: 13.9 us -> 11.5 us
    all_gather x2 -> x1, waiting for transfers between devices: 125 us -> 73.6 us  [local(): full_conv = (lax.all_gather(conv_weight[0], 'batch', axis=0, tiled=True),)]
    ppermute x7 -> x6, waiting for transfers between devices: 18.7 us -> 22.8 us  [moved(): lax.ppermute(value, 'section', [(at, (at + steps) % count) for at in rang...]
    pallas_call x3 -> x2, Pallas kernels: 26.2 us -> 22.4 us  [by_tap(): pl.pallas_call(kernel, grid=(TAPS,), in_specs=[whole(value.shape) for val...]
    ppermute x7 -> x6, starting transfers between devices: 12 us -> 9.13 us  [moved(): lax.ppermute(value, 'section', [(at, (at + steps) % count) for at in rang...]
    slice x1 -> x0, local copies, waits for them, and re-layouts: 2.54 us -> none  [local(): conv_weight[0, :, begin:begin + half]]
  transfers between devices with their start and end apart: 9 -> 7, of which waited for: 6 -> 5; matrix products, arithmetic and copies ran while one was open for 11% -> 13% of each run, Pallas kernels for 13% -> 15%
where the time goes in v4:
time: 174 us; the launch traced here: 173 us
  waiting for transfers between devices  97.2 us (56%)
  Pallas kernels  25.9 us (15%)
  between operations  14.3 us (8%)
  other arithmetic  11.5 us (7%)
  matrix products  9.47 us (5%)
  starting transfers between devices  9.17 us (5%)
  local copies, waits for them, and re-layouts  5.74 us (3%)
    all_gather x1, waiting for transfers between devices, local(): full_conv = (lax.all_gather(conv_weight[0], 'batch', axis=0, tiled=True),)  73.6 us
    ppermute x6, waiting for transfers between devices, moved(): lax.ppermute(value, 'section', [(at, (at + steps) % count) for at in rang...  22.8 us
    pallas_call x2, Pallas kernels, by_tap(): pl.pallas_call(kernel, grid=(TAPS,), in_specs=[whole(value.shape) for val...  22.4 us
    ppermute x6, starting transfers between devices, moved(): lax.ppermute(value, 'section', [(at, (at + steps) % count) for at in rang...  9.13 us
    pallas_call x1, Pallas kernels, adjoint_from(): pl.pallas_call(finish_back, out_shape=jax.ShapeDtypeStruct(upstream.shape...  3.5 us
  transfers between devices with their start and end apart: 7, of which 5 were waited for; matrix products, arithmetic and copies ran while one was open for 13% of the time, Pallas kernels for 15%

profile of v4, /device:TPU:0, one launch (start us, length us, event | category | flops | bytes accessed | tf_op | source)
XLA Modules:
  0.0 173.4 jit_solution(16569888909961346825)
XLA Ops:
  12.1 1.3 slice_bitcast_fusion.8
  13.7 1.4 fusion.12
  15.3 1.1 fusion.4
  16.5 1.6 fusion.40
  19.7 3.0 %collective-permute-start = (bf16[2,128,1024]{2,1,0:T(8,128)(2,1)}, bf16[2,128,1024]{2,1,0:T(8,128)(2,1)}, u32[]{:S(2)}, u32[]{:S(2)}) collective-permute-start(bf16[2,128,1024]{2,1,0:T(8,128)(2,1)} %pad_maximum_fusion.1), channel_id=1, source_target_pairs={{0,16},{16,0},{1,17},{17,1},{2,18},{18,2},{3,19},{19,3},{4,20},{20... | collective-permute-start | bytes 1572872 | tf_op jit(solution)/shard_map/ppermute | solution.py:256
  23.3 2.3 %convolution_convert_fusion = bf16[384,1024]{1,0:T(8,128)(2,1)} fusion(bf16[384,1536]{1,0:T(8,128)(2,1)S(1)} %bitcast.91, bf16[1536,1024]{1,0:T(8,128)(2,1)S(1)} %copy-done), kind=kOutput, calls=%fused_computation.4 | convolution fusion | flops 1208352768 | bytes 5111808 | tf_op jit(solution)/shard_map/dot_general | solution.py:345
  25.8 2.9 %fusion.scaling_ref = f32[2,2048]{1,0:T(2,128)S(1)} fusion(bf16[1,1024,2048]{2,1,0:T(8,128)(2,1)} %param.22, f32[2,512]{1,0:T(2,128)S(1)} %get-tuple-element.77, f32[2,512]{1,0:T(2,128)S(1)} %get-tuple-element.76), kind=kOutput, calls=%fused_computation | convolution fusion | flops 8400896 | bytes 4218880 | tf_op jit(solution)/shard_map/dot_general | solution.py:344
  28.7 7.0 %collective-permute-done = bf16[2,128,1024]{2,1,0:T(8,128)(2,1)} collective-permute-done((bf16[2,128,1024]{2,1,0:T(8,128)(2,1)}, bf16[2,128,1024]{2,1,0:T(8,128)(2,1)}, u32[]{:S(2)}, u32[]{:S(2)}) %collective-permute-start) | collective-permute-done | bytes 524320 | tf_op jit(solution)/shard_map/ppermute | solution.py:256
  35.7 1.2 add_convert_fusion
  37.7 73.6 %all-gather.3.cloned.1.call-done = bf16[1,9216,1024]{2,1,0:T(8,128)(2,1)} async-done(((bf16[1,576,1024]{2,1,0:T(8,128)(2,1)}), bf16[1,9216,1024]{2,1,0:T(8,128)(2,1)}) %all-gather.3.cloned.1.call-update) | async-done | bytes 18874384 | tf_op jit(solution)/shard_map/all_gather | solution.py:319
  111.3 9.9 %conditional.2 = (bf16[128,1024]{1,0:T(8,128)(2,1)}) conditional(s32[]{:T(128)} %convert_element_type.58, (bf16[128,1024]{1,0:T(8,128)(2,1)}, bf16[9216,1024]{1,0:T(8,128)(2,1)}) %tuple.59, (bf16[128,1024]{1,0:T(8,128)(2,1)S(1)}, f32[2,2048]{1,0:T(2,128)S(1)}, bf16[9216,1024]{1,0:T(8,128)(2,1)}) %tuple.60), branch_computations={%region_1.2_spmd, %region_2.3_spmd} | conditional | flops 2415919104 | bytes 18874376 | solution.py:267
  111.3 9.9 %branch_1_fun.2 = bf16[128,1024]{1,0:T(8,128)(2,1)} custom-call(bf16[128,1024]{1,0:T(8,128)(2,1)S(1)} %get-tuple-element.32.feature_ref, f32[2,2048]{1,0:T(2,128)S(1)} %get-tuple-element.33.scaling_ref, bf16[9216,1024]{1,0:T(8,128)(2,1)} %get-tuple-element.34.refs_0_), custom_call_target="tpu_custom_call" | custom-call | flops 2415919104 | bytes 18874368 | tf_op jit(solution)/shard_map/cond/branch_1_fun/pallas_call | solution.py:213
  121.2 2.3 %collective-permute-start.1 = (bf16[128,1024]{1,0:T(8,128)(2,1)}, bf16[128,1024]{1,0:T(8,128)(2,1)}, u32[]{:S(2)}, u32[]{:S(2)}) collective-permute-start(bf16[128,1024]{1,0:T(8,128)(2,1)} %get-tuple-element.88.slope_ref), channel_id=1, source_target_pairs={{0,16},{16,0},{1,17},{17,1},{2,18},{18,2},{3,19},{19,3},{4,20},{20... | collective-permute-start | bytes 786440 | tf_op jit(solution)/shard_map/ppermute | solution.py:256
  123.6 7.0 %collective-permute-done.1.feature_ref = bf16[128,1024]{1,0:T(8,128)(2,1)} collective-permute-done((bf16[128,1024]{1,0:T(8,128)(2,1)}, bf16[128,1024]{1,0:T(8,128)(2,1)}, u32[]{:S(2)}, u32[]{:S(2)}) %collective-permute-start.1) | collective-permute-done | bytes 262176 | tf_op jit(solution)/shard_map/ppermute | solution.py:256
  130.6 3.5 %shard_map.113 = bf16[128,1024]{1,0:T(8,128)(2,1)} custom-call(bf16[128,1024]{1,0:T(8,128)(2,1)} %get-tuple-element.56.upstream_ref, bf16[128,1024]{1,0:T(8,128)(2,1)} %collective-permute-done.1.feature_ref, f32[2,2048]{1,0:T(2,128)S(1)} %fusion.scaling_ref, bf16[128,1024]{1,0:T(8,128)(2,1)} %get-tuple-element.88.slope_ref), custom_call_target="tpu_custom_call" | custom-call | tf_op jit(solution)/shard_map/pallas_call | solution.py:248
  134.1 1.7 %collective-permute-start.2 = (bf16[128,1024]{1,0:T(8,128)(2,1)}, bf16[128,1024]{1,0:T(8,128)(2,1)}, u32[]{:S(2)}, u32[]{:S(2)}) collective-permute-start(bf16[128,1024]{1,0:T(8,128)(2,1)} %shard_map.113), channel_id=1, source_target_pairs={{0,16},{16,0},{1,17},{17,1},{2,18},{18,2},{3,19},{19,3},{4,20},{20... | collective-permute-start | bytes 786440 | tf_op jit(solution)/shard_map/ppermute | solution.py:256
  135.8 6.5 %collective-permute-done.2 = bf16[128,1024]{1,0:T(8,128)(2,1)} collective-permute-done((bf16[128,1024]{1,0:T(8,128)(2,1)}, bf16[128,1024]{1,0:T(8,128)(2,1)}, u32[]{:S(2)}, u32[]{:S(2)}) %collective-permute-start.2) | collective-permute-done | bytes 262176 | tf_op jit(solution)/shard_map/ppermute | solution.py:256
  142.4 12.7 %conditional.3 = (bf16[128,1024]{1,0:T(8,128)(2,1)}) conditional(s32[]{:T(128)} %convert_element_type.58, (bf16[128,1024]{1,0:T(8,128)(2,1)}, f32[2,2048]{1,0:T(2,128)S(1)}, bf16[9216,1024]{1,0:T(8,128)(2,1)}) %tuple.61, (bf16[128,1024]{1,0:T(8,128)(2,1)}, bf16[128,1024]{1,0:T(8,128)(2,1)S(1)}, f32[2,2048]{1,0:T(2,128)S(1)}, ...), branch_computations={%region_3.4_spmd, %region_4.5_spmd} | conditional | flops 2415919104 | bytes 18874376 | solution.py:274
  142.6 12.5 %branch_1_fun.3 = bf16[128,1024]{1,0:T(8,128)(2,1)} custom-call(bf16[128,1024]{1,0:T(8,128)(2,1)} %get-tuple-element.38.upstream_ref, bf16[128,1024]{1,0:T(8,128)(2,1)S(1)} %get-tuple-element.39.feature_ref, f32[2,2048]{1,0:T(2,128)S(1)} %get-tuple-element.40.scaling_ref, bf16[9216,1024]{1,0:T(8,128)(2,1)} %get-tuple-element.41.refs_0_), custom_call_target="tpu_custom_call" | custom-call | flops 2415919104 | bytes 18874368 | tf_op jit(solution)/shard_map/cond/branch_1_fun/pallas_call | solution.py:213
  155.1 1.0 bitcast_convert_fusion
  156.1 1.7 fusion.2
  158.1 2.1 %collective-permute-start.5 = (f32[2,2]{0,1:T(2,128)S(1)}, f32[2,2]{0,1:T(2,128)S(1)}, u32[]{:S(2)}, u32[]{:S(2)}) collective-permute-start(f32[2,2]{0,1:T(2,128)S(1)} %pad_maximum_fusion.3), channel_id=1, source_target_pairs={{0,16},{16,0},{1,17},{17,1},{2,18},{18,2},{3,19},{19,3},{4,20},{20... | collective-permute-start | bytes 56 | tf_op jit(solution)/shard_map/ppermute | solution.py:256
  160.2 2.2 %collective-permute-done.5 = f32[2,2]{0,1:T(2,128)S(1)} collective-permute-done((f32[2,2]{0,1:T(2,128)S(1)}, f32[2,2]{0,1:T(2,128)S(1)}, u32[]{:S(2)}, u32[]{:S(2)}) %collective-permute-start.5) | collective-permute-done | bytes 48 | tf_op jit(solution)/shard_map/ppermute | solution.py:256
  163.1 2.5 %fusion.16 = f32[128,1536]{1,0:T(8,128)S(1)} fusion(bf16[1024,1536]{1,0:T(8,128)(2,1)} %param.23, bf16[128,1024]{1,0:T(8,128)(2,1)S(1)} %collective-permute-done.3, bf16[128,1024]{1,0:T(8,128)(2,1)} %get-tuple-element.89, pred[]{:T(512)S(6)} %eq.4), kind=kOutput, calls=%fused_computation.35 | convolution fusion | flops 402784256 | bytes 4456449 | tf_op jit(solution)/shard_map/dot_general | solution.py:361
  (67 shorter events, 10.2 us)
Async XLA Ops:
  7.2 11.0 %copy-start = (bf16[1536,1024]{1,0:T(8,128)(2,1)S(1)}, bf16[1536,1024]{1,0:T(8,128)(2,1)}, u32[]{:S(2)}) copy-start(bf16[1536,1024]{1,0:T(8,128)(2,1)} %param.20) | copy-start | bytes 9437188
  7.2 6.3 %copy-start.1 = (bf16[2,64,1536]{2,1,0:T(8,128)(2,1)S(1)}, bf16[2,64,1536]{2,1,0:T(8,128)(2,1)}, u32[]{:S(2)}) copy-start(bf16[2,64,1536]{2,1,0:T(8,128)(2,1)} %param.14) | copy-start | bytes 1179652
  7.2 104.1 %all-gather.3.cloned.1.call-start = ((), (), s32[]{:S(2)}) async-start(), calls=%async_computation | async-start | bytes 20054016 | tf_op jit(solution)/shard_map/all_gather | solution.py:319
  7.9 5.8 %copy-start.8 = (bf16[2,64,1536]{2,1,0:T(8,128)(2,1)S(1)}, bf16[2,64,1536]{2,1,0:T(8,128)(2,1)}, u32[]{:S(2)}) copy-start(bf16[2,64,1536]{2,1,0:T(8,128)(2,1)} %param.16) | copy-start | bytes 1179652
  9.7 5.4 %copy-start.12 = (f32[2]{0:T(128)}, f32[2]{0:T(128)S(1)}, u32[]{:S(2)}) copy-start(f32[2]{0:T(128)S(1)} %get-tuple-element.84) | copy-start | bytes 28
  9.7 5.4 %copy-start.14 = (f32[2]{0:T(128)}, f32[2]{0:T(128)S(1)}, u32[]{:S(2)}) copy-start(f32[2]{0:T(128)S(1)} %get-tuple-element.85) | copy-start | bytes 28
  13.4 1.9 %copy-start.2 = (bf16[1024,1536]{1,0:T(8,128)(2,1)S(1)}, bf16[1024,1536]{1,0:T(8,128)(2,1)}, u32[]{:S(2)}) copy-start(bf16[1024,1536]{1,0:T(8,128)(2,1)} %param.23) | copy-start | bytes 9437188
  13.7 2.8 %copy-start.9 = (bf16[2,64,1536]{2,1,0:T(8,128)(2,1)S(1)}, bf16[2,64,1536]{2,1,0:T(8,128)(2,1)}, u32[]{:S(2)}) copy-start(bf16[2,64,1536]{2,1,0:T(8,128)(2,1)} %param.15) | copy-start | bytes 1179652
  16.5 2.2 %copy-start.4 = (bf16[1,128,1024]{2,1,0:T(8,128)(2,1)}, bf16[1,128,1024]{2,1,0:T(8,128)(2,1)S(1)}, u32[]{:S(2)}) copy-start(bf16[1,128,1024]{2,1,0:T(8,128)(2,1)S(1)} %fusion.4) | copy-start | bytes 786436
  18.7 0.9 copy-start.6
  19.7 16.0 %collective-permute-start = (bf16[2,128,1024]{2,1,0:T(8,128)(2,1)}, bf16[2,128,1024]{2,1,0:T(8,128)(2,1)}, u32[]{:S(2)}, u32[]{:S(2)}) collective-permute-start(bf16[2,128,1024]{2,1,0:T(8,128)(2,1)} %pad_maximum_fusion.1), channel_id=1, source_target_pairs={{0,16},{16,0},{1,17},{17,1},{2,18},{18,2},{3,19},{19,3},{4,20},{20... | collective-permute-start | bytes 1572872 | tf_op jit(solution)/shard_map/ppermute | solution.py:256
  23.2 2.4 %copy-start.16 = (s32[2]{0:T(128)S(1)}, s32[2]{0:T(128)}, u32[]{:S(2)}) copy-start(s32[2]{0:T(128)} %param.19) | copy-start | bytes 28
  25.6 10.1 %copy-start.5 = (bf16[1,128,1024]{2,1,0:T(8,128)(2,1)S(1)}, bf16[1,128,1024]{2,1,0:T(8,128)(2,1)}, u32[]{:S(2)}) copy-start(bf16[1,128,1024]{2,1,0:T(8,128)(2,1)} %copy-done.4) | copy-start | bytes 786436
  25.6 130.5 %collective-permute-start.4 = (bf16[384,1024]{1,0:T(8,128)(2,1)}, bf16[384,1024]{1,0:T(8,128)(2,1)}, u32[]{:S(2)}, u32[]{:S(2)}) collective-permute-start(bf16[384,1024]{1,0:T(8,128)(2,1)} %convolution_convert_fusion), channel_id=1, source_target_pairs={{0,16},{16,0},{1,17},{17,1},{2,18},{18,2},{3,19},{19,3},{4,20},{20... | collective-permute-start | bytes 2359304 | tf_op jit(solution)/shard_map/ppermute | solution.py:256
  25.6 10.1 %copy-start.7 = (bf16[1,128,1024]{2,1,0:T(8,128)(2,1)S(1)}, bf16[1,128,1024]{2,1,0:T(8,128)(2,1)}, u32[]{:S(2)}) copy-start(bf16[1,128,1024]{2,1,0:T(8,128)(2,1)} %copy-done.6) | copy-start | bytes 786436
  121.2 9.4 %collective-permute-start.1 = (bf16[128,1024]{1,0:T(8,128)(2,1)}, bf16[128,1024]{1,0:T(8,128)(2,1)}, u32[]{:S(2)}, u32[]{:S(2)}) collective-permute-start(bf16[128,1024]{1,0:T(8,128)(2,1)} %get-tuple-element.88.slope_ref), channel_id=1, source_target_pairs={{0,16},{16,0},{1,17},{17,1},{2,18},{18,2},{3,19},{19,3},{4,20},{20... | collective-permute-start | bytes 786440 | tf_op jit(solution)/shard_map/ppermute | solution.py:256
  134.1 8.3 %collective-permute-start.2 = (bf16[128,1024]{1,0:T(8,128)(2,1)}, bf16[128,1024]{1,0:T(8,128)(2,1)}, u32[]{:S(2)}, u32[]{:S(2)}) collective-permute-start(bf16[128,1024]{1,0:T(8,128)(2,1)} %shard_map.113), channel_id=1, source_target_pairs={{0,16},{16,0},{1,17},{17,1},{2,18},{18,2},{3,19},{19,3},{4,20},{20... | collective-permute-start | bytes 786440 | tf_op jit(solution)/shard_map/ppermute | solution.py:256
  142.4 15.6 %copy-start.10 = (f32[2]{0:T(128)S(1)}, f32[2]{0:T(128)}, u32[]{:S(2)}) copy-start(f32[2]{0:T(128)} %get-tuple-element.52) | copy-start | bytes 28
  142.4 15.6 %copy-start.11 = (f32[2]{0:T(128)S(1)}, f32[2]{0:T(128)}, u32[]{:S(2)}) copy-start(f32[2]{0:T(128)} %param.18) | copy-start | bytes 28
  142.4 15.6 %copy-start.13 = (f32[2]{0:T(128)S(1)}, f32[2]{0:T(128)}, u32[]{:S(2)}) copy-start(f32[2]{0:T(128)} %copy-done.12) | copy-start | bytes 28
  142.4 15.7 %copy-start.15 = (f32[2]{0:T(128)S(1)}, f32[2]{0:T(128)}, u32[]{:S(2)}) copy-start(f32[2]{0:T(128)} %copy-done.14) | copy-start | bytes 28
  155.0 8.0 %collective-permute-start.3 = (bf16[128,1024]{1,0:T(8,128)(2,1)}, bf16[128,1024]{1,0:T(8,128)(2,1)S(1)}, u32[]{:S(2)}, u32[]{:S(2)}) collective-permute-start(bf16[128,1024]{1,0:T(8,128)(2,1)} %get-tuple-element.89), channel_id=1, source_target_pairs={{0,16},{16,0},{1,17},{17,1},{2,18},{18,2},{3,19},{19,3},{4,20},{20... | collective-permute-start | bytes 786440 | tf_op jit(solution)/shard_map/ppermute | solution.py:256
  158.1 4.3 %collective-permute-start.5 = (f32[2,2]{0,1:T(2,128)S(1)}, f32[2,2]{0,1:T(2,128)S(1)}, u32[]{:S(2)}, u32[]{:S(2)}) collective-permute-start(f32[2,2]{0,1:T(2,128)S(1)} %pad_maximum_fusion.3), channel_id=1, source_target_pairs={{0,16},{16,0},{1,17},{17,1},{2,18},{18,2},{3,19},{19,3},{4,20},{20... | collective-permute-start | bytes 56 | tf_op jit(solution)/shard_map/ppermute | solution.py:256
  163.1 2.6 %copy-start.3 = (f32[2,64,1536]{2,1,0:T(8,128)S(1)}, f32[2,64,1536]{2,1,0:T(8,128)}, u32[]{:S(2)}) copy-start(f32[2,64,1536]{2,1,0:T(8,128)} %get-tuple-element.54) | copy-start | bytes 2359300
Sparse Core Ops, SparseCore 0:
  9.6 101.6 all-gather.2
